TPU v7x, 32 devices: a whole 2x2x4 slice. The times are simulated.
32 devices in a mesh: grp: 2 (over y), dev: 16 (over z, x, core).
Axes of the slice: x: 2, y: 2, z: 4, core: 2. Of those that a mesh axis runs over, the one named last changes fastest.
Arguments:
- offsets: float32 [128, 3, 512], P(('grp', 'dev')), may hold values from 0 to 1
- sketch: bfloat16 [128, 512, 256], P(('grp', 'dev')), may hold values from -6 to 6
- pattern: int32 [128, 6], P(('grp', 'dev')), may hold values 0 or 1
- point_order: int32 [128, 512], P(('grp', 'dev')), may hold values from 0 to 511, each once within a row
Outputs:
- basis: bfloat16 [128, 512, 256], P(('grp', 'dev'))
- basis_factor: float32 [128, 256, 256], P(('grp', 'dev'))
Inputs may be any that keep to these rules, and one draw needn't show every extreme that they name: `point_order`: each row is a permutation of 0 .. 511.
All inputs are finite; a program needn't handle non-finite values. No bound on the sum of `pattern` on one device may be relied on, other than what follows from the above.
Results may differ from a plain program's by a relative error of at most 0.0082.
Values may be sent and summed in bfloat16 or wider, within the bound.
No kernel may reach another device: no remote copies, remote signals or barrier semaphores. Data moves between devices by JAX's collectives and lax.ppermute only.
A program may use at most 64 MiB of HBM per device.

v0:
```python
import functools
import math

import numpy as np
import jax
import jax.numpy as jnp
from jax import lax
from jax.experimental import pallas as pl
from jax.experimental.pallas import tpu as pltpu
from jax.sharding import PartitionSpec as P

W = 4
AXES = ("grp", "dev")
f32 = jnp.float32
bf16 = jnp.bfloat16

wave_number = 40.0
decay_length = 4.0
softening = 0.5
turns = wave_number / (2.0 * math.pi)

SINE = (4.44288292, -7.30824569, 3.60635423, -0.84611167, 0.10982452)


def passed_along(array, by):
    peers = lax.axis_size(AXES)
    pairs = [(i, i + by) for i in range(peers) if 0 <= i + by < peers]
    return lax.ppermute(array, AXES, pairs)


def offset_table(reach):
    return [-value for value in range(reach, 1, -1)] + list(range(2, reach + 1))


def kernel_values(turn_squared, points):
    turn = turn_squared * lax.rsqrt(turn_squared)
    part = turn - jnp.round(turn)
    square = part * part
    sine = f32(SINE[-1])
    for value in SINE[-2::-1]:
        sine = sine * square + f32(value)
    sine = sine * part
    decay = jnp.exp2(
        turn * f32(-math.log2(math.e) / (decay_length * turns)) + f32(math.log2(turns / math.sqrt(points)))
    )
    level = decay * pltpu.reciprocal(turn + f32(softening * turns), approx=True)
    return level - level * (sine * sine)


def pieces(x):
    high = x.astype(bf16).astype(f32)
    middle = (x - high).astype(bf16).astype(f32)
    low = (x - high - middle).astype(bf16).astype(f32)
    return high, middle, low


def turn_squares(target, source, distance):
    row = lax.broadcasted_iota(jnp.int32, target.shape, 0)
    half = distance.astype(f32) * f32(0.5)

    def shifted(x, along):
        moved = x + jnp.where(row == 0, along, jnp.where(row < 3, f32(-0.5), f32(0)))
        moved = moved * f32(turns)
        return moved, jnp.sum(moved * moved, axis=0, keepdims=True)

    left, left_norm = shifted(target, -half - f32(0.5))
    right, right_norm = shifted(source, half - f32(0.5))
    left = jnp.where(row == 3, left_norm, jnp.where(row == 4, f32(1), left))
    right = jnp.where(row == 4, right_norm, jnp.where(row == 3, f32(1), f32(-2) * right))
    lh, lm, ll = pieces(left)
    rh, rm, rl = pieces(right)
    a = jnp.concatenate([lh, lh, lm, lm, lh, ll, lm, ll], axis=0).astype(bf16)
    b = jnp.concatenate([rh, rm, rh, rm, rl, rh, rl, rm], axis=0).astype(bf16)
    return contract(a, b, 0, 0)


def halves(x):
    hi = x.astype(bf16)
    return hi, (x - hi.astype(f32)).astype(bf16)

def contract(a, b, da, db):
    return lax.dot_general(a, b, (((da,), (db,)), ((), ())), preferred_element_type=f32)

def lane_of(x, lane):
    return jnp.broadcast_to(x[:, lane:lane + 1], x.shape)

def factor_panel(rows, ups, first, panel, micro):
    half = first // 128
    base = first % 128
    lanes = lax.broadcasted_iota(jnp.int32, (8, 128), 1)
    for start in range(0, panel, micro):
        lane0 = base + start
        inside = (lanes >= lane0) & (lanes < lane0 + micro)
        raw = [rows[half, 8 * (start + j):8 * (start + j) + 8, :] for j in range(micro)]
        other = [rows[1 - half, 8 * (start + j):8 * (start + j) + 8, :] for j in range(micro)]
        a = [[lane_of(raw[i], lane0 + k) for k in range(i + 1)] for i in range(micro)]
        low = [[None] * micro for _ in range(micro)]
        inv = [None] * micro
        for k in range(micro):
            inv[k] = lax.rsqrt(a[k][k])
            for i in range(k + 1, micro):
                low[i][k] = a[i][k] * inv[k]
            for i in range(k + 1, micro):
                for m in range(k + 1, i + 1):
                    a[i][m] = a[i][m] - low[i][k] * low[m][k]
        solved = [jnp.where(inside, jnp.where(lanes == lane0 + j, f32(1), f32(0)), raw[j]) for j in range(micro)]
        for k in range(micro):
            raw[k] = raw[k] * inv[k]
            solved[k] = solved[k] * inv[k]
            other[k] = other[k] * inv[k]
            for i in range(k + 1, micro):
                raw[i] = raw[i] - low[i][k] * raw[k]
                solved[i] = solved[i] - low[i][k] * solved[k]
                other[i] = other[i] - low[i][k] * other[k]
        for j in range(micro):
            at = slice(8 * (start + j), 8 * (start + j) + 8)
            ups[at, :] = raw[j]
            rows[half, at, :] = solved[j]
            rows[1 - half, at, :] = other[j]
        for i in range(start + micro, panel):
            at = slice(8 * i, 8 * i + 8)
            x = jnp.where(inside, f32(0), rows[half, at, :])
            y = rows[1 - half, at, :]
            tx = ty = None
            for j in range(micro):
                c = lane_of(raw[j], base + i)
                tx = c * solved[j] if tx is None else tx + c * solved[j]
                ty = c * other[j] if ty is None else ty + c * other[j]
            rows[half, at, :] = x - tx
            rows[1 - half, at, :] = y - ty

def chol_body(s_ref, order_ref, basis_ref, factor_ref, mat, inv_ref, rows, ups, *, panel, micro):
    count, points, width = s_ref.shape
    row_id = lax.broadcasted_iota(jnp.int32, (width, width), 0)
    col_id = lax.broadcasted_iota(jnp.int32, (width, width), 1)
    for c in range(count):
        hi, lo = halves(s_ref[c])
        gram = contract(hi, hi, 0, 0)
        cross = contract(hi, lo, 0, 0)
        gram = gram + (cross + cross.T)
        shift = f32(0.01) * jnp.sum(jnp.where(row_id == col_id, gram, f32(0))) / f32(width) + f32(1e-5)
        mat[c] = gram + jnp.where(row_id == col_id, shift, f32(0))
    for first in range(0, width, panel):
        half = first // 128
        base = first % 128
        for c in range(count):
            for h in range(2):
                for t in range(0, panel, 8):
                    tile = mat[c, first + t:first + t + 8, 128 * h:128 * h + 128]
                    rows[h, pl.ds(8 * t + c, 8, stride=8), :] = tile
        factor_panel(rows, ups, first, panel, micro)
        prow = lax.broadcasted_iota(jnp.int32, (panel, 128), 0) + base
        pcol = lax.broadcasted_iota(jnp.int32, (panel, 128), 1)
        for c in range(count):
            z = [rows[h, pl.ds(c, panel, stride=8), :] for h in range(2)]
            u = ups[pl.ds(c, panel, stride=8), :]
            u = jnp.where(pcol >= prow, u, f32(0))
            wz = jnp.where((pcol <= prow) | (pcol >= base + panel), z[half], f32(0))
            w = jnp.where(pcol <= prow, z[half], f32(0))
            z[half] = wz
            factor_ref[c, first:first + panel, 128 * half:128 * half + 128] = u
            factor_ref[c, first:first + panel, 128 * (1 - half):128 * (1 - half) + 128] = z[1] if half == 0 else jnp.zeros_like(u)
            inv_ref[c, first:first + panel, 128 * half:128 * half + 128] = w
            inv_ref[c, first:first + panel, 128 * (1 - half):128 * (1 - half) + 128] = z[0] if half == 1 else jnp.zeros_like(u)
            rest = first + panel
            if rest < width:
                zz = jnp.concatenate(z, axis=1)
                hi, lo = halves(zz)
                left = jnp.concatenate([hi, hi, lo], axis=0)
                right = jnp.concatenate([hi, lo, hi], axis=0)
                off = (rest // 128) * 128
                prod = contract(left[:, off:], right, 0, 0)[rest - off:, :]
                old = mat[c, rest:, :]
                cc = col_id[rest:, :]
                old = jnp.where((cc >= first) & (cc < rest), f32(0), old)
                mat[c, rest:, :] = old - prod
    for c in range(count):
        hi, lo = halves(s_ref[c])
        wh, wl = halves(inv_ref[c])
        b = contract(jnp.concatenate([hi, hi, lo], axis=1), jnp.concatenate([wh, wl, wh], axis=1), 1, 1)
        b = b.astype(bf16)
        order = order_ref[c:c + 1, :].astype(f32)
        order_t = jnp.broadcast_to(order, (128, points)).T
        place = lax.broadcasted_iota(jnp.int32, (points, 128), 1).astype(f32)
        pick = jnp.concatenate([jnp.where(order_t == place + f32(128 * q), f32(1), f32(0)).astype(bf16) for q in range(points // 128)], axis=1)
        basis_ref[c] = jnp.dot(pick, b, preferred_element_type=f32).astype(bf16)

def chol_call(s, order, panel=64, micro=8, interpret=False):
    count, points, width = s.shape
    return pl.pallas_call(
        functools.partial(chol_body, panel=panel, micro=micro),
        out_shape=(jax.ShapeDtypeStruct((count, points, width), bf16), jax.ShapeDtypeStruct((count, width, width), f32)),
        scratch_shapes=[pltpu.VMEM((count, width, width), f32), pltpu.VMEM((count, width, width), f32),
            pltpu.VMEM((2, 8 * panel, 128), f32), pltpu.VMEM((8 * panel, 128), f32)],
        compiler_params=pltpu.CompilerParams(vmem_limit_bytes=48 * 2**20),
    )(s, order)


def active(first, pattern, cluster, column, distance, total):
    source = first + cluster + distance
    return (pattern != 0) & (source >= 0) & (source < total)


def blocks_body(cl_ref, co_ref, di_ref, first_ref, pattern_ref, prev_ref, own_ref, next_ref, out_ref, window, *, total):
    step = pl.program_id(0)
    count, _, points = own_ref.shape
    first = first_ref[0]

    @pl.when(step == 0)
    def _():
        window[...] = jnp.zeros_like(window)
        for slot in range(3 * count):
            ref = (prev_ref, own_ref, next_ref)[slot // count]
            index = (first + (slot - count)).astype(f32)
            xs = ref[slot % count]
            along = (xs[0:1] + index) - index
            window[slot, 0:1, :] = along
            window[slot, 1:3, :] = xs[1:3]

    cluster = cl_ref[step]
    column = co_ref[step]
    distance = di_ref[step]

    @pl.when(active(first, pattern_ref[cluster, column], cluster, column, distance, total))
    def _():
        squares = turn_squares(window[count + cluster], window[count + cluster + distance], distance)
        out_ref[0] = kernel_values(squares, points).astype(bf16)


def blocks_of(pairs, first, pattern, prev, own, after, total):
    count, _, points = own.shape
    table = offset_table(W)
    tabs = [jnp.asarray(np.array(x, np.int32)) for x in zip(*[(c, k, table[k]) for c, k in pairs])]
    whole = pl.BlockSpec(memory_space=pltpu.VMEM)
    return pl.pallas_call(
        functools.partial(blocks_body, total=total),
        grid_spec=pltpu.PrefetchScalarGridSpec(
            num_scalar_prefetch=5,
            grid=(len(pairs),),
            in_specs=[whole, whole, whole],
            out_specs=pl.BlockSpec((1, points, points), lambda i, *_: (i, 0, 0)),
            scratch_shapes=[pltpu.VMEM((3 * count, 8, points), f32)],
        ),
        out_shape=jax.ShapeDtypeStruct((len(pairs), points, points), bf16),
        compiler_params=pltpu.CompilerParams(vmem_limit_bytes=32 * 2**20),
        name="blocks",
    )(*tabs, first, pattern, prev, own, after)


def samples_body(first_ref, pattern_ref, k_ref, prev_ref, own_ref, next_ref, out_ref, *, total, count, table):
    cluster = pl.program_id(0)
    first = first_ref[0]
    for column, distance in enumerate(table):
        if column == 0:
            out_ref[...] = jnp.zeros_like(out_ref)

        @pl.when(active(first, pattern_ref[cluster, column], cluster, column, distance, total))
        def _():
            slot = cluster + distance

            def add(ref, index):
                out_ref[0] += jnp.dot(k_ref[column], ref[index], preferred_element_type=f32)

            @pl.when(slot < 0)
            def _():
                add(prev_ref, slot + count)

            @pl.when((slot >= 0) & (slot < count))
            def _():
                add(own_ref, slot)

            @pl.when(slot >= count)
            def _():
                add(next_ref, slot - count)


def samples_of(first, pattern, blocks, prev, own, after, total):
    count, points, width = own.shape
    table = offset_table(W)
    whole = pl.BlockSpec(memory_space=pltpu.VMEM)
    return pl.pallas_call(
        functools.partial(samples_body, total=total, count=count, table=table),
        grid_spec=pltpu.PrefetchScalarGridSpec(
            num_scalar_prefetch=2,
            grid=(count,),
            in_specs=[pl.BlockSpec((len(table), points, points), lambda c, *_: (c, 0, 0)), whole, whole, whole],
            out_specs=pl.BlockSpec((1, points, width), lambda c, *_: (c, 0, 0)),
        ),
        out_shape=jax.ShapeDtypeStruct((count, points, width), f32),
        compiler_params=pltpu.CompilerParams(vmem_limit_bytes=40 * 2**20),
        name="samples",
    )(first, pattern, blocks, prev, own, after)


def body(offsets, sketch, pattern, point_order):
    count = offsets.shape[0]
    total = count * lax.axis_size(AXES)
    first = (lax.axis_index(AXES) * count).astype(jnp.int32).reshape(1)
    prev_offsets = passed_along(offsets, 1)
    next_offsets = passed_along(offsets, -1)
    prev_sketch = passed_along(sketch, 1)
    next_sketch = passed_along(sketch, -1)
    pairs = [(c, k) for c in range(count) for k in range(len(offset_table(W)))]
    blocks = blocks_of(pairs, first, pattern, prev_offsets, offsets, next_offsets, total)
    samples = samples_of(first, pattern, blocks, prev_sketch, sketch, next_sketch, total)
    return chol_call(samples, point_order)


def solution(mesh):
    rows = P(AXES, None, None)
    flat = P(AXES, None)
    return jax.shard_map(
        body,
        mesh=mesh,
        in_specs=(rows, rows, flat, flat),
        out_specs=(rows, rows),
        check_vma=False,
    )
```

profile of v0, /device:TPU:1, one launch (start us, length us, event | category | flops | bytes accessed | tf_op | source)
XLA Modules:
  0.0 90.0 jit_solution(8342566275531038556)
XLA Ops:
  0.6 0.0 copy-start.1
  0.6 4.6 %collective-permute-start.2 = (bf16[4,512,256]{2,1,0:T(8,128)(2,1)}, bf16[4,512,256]{2,1,0:T(8,128)(2,1)S(1)}, u32[]{:S(2)}, u32[]{:S(2)}) collective-permute-start(bf16[4,512,256]{2,1,0:T(8,128)(2,1)} %own_ref.2), channel_id=1, source_target_pairs={{0,1},{1,2},{2,3},{3,4},{4,5},{5,6},{6,7},{7,8},{8,9},{9,10},{10,1... | collective-permute-start | bytes 3145736 | tf_op jit(solution)/shard_map/ppermute | solution.py:28
  5.3 1.9 %collective-permute-start.3 = (bf16[4,512,256]{2,1,0:T(8,128)(2,1)}, bf16[4,512,256]{2,1,0:T(8,128)(2,1)S(1)}, u32[]{:S(2)}, u32[]{:S(2)}) collective-permute-start(bf16[4,512,256]{2,1,0:T(8,128)(2,1)} %own_ref.2), channel_id=1, source_target_pairs={{1,0},{2,1},{3,2},{4,3},{5,4},{6,5},{7,6},{8,7},{9,8},{10,9},{11,1... | collective-permute-start | bytes 3145736 | tf_op jit(solution)/shard_map/ppermute | solution.py:28
  7.2 0.8 copy.9.own_ref
  8.0 1.9 %collective-permute-start.1 = (f32[4,3,512]{2,1,0:T(4,128)S(1)}, f32[4,3,512]{2,1,0:T(4,128)S(1)}, u32[]{:S(2)}, u32[]{:S(2)}) collective-permute-start(f32[4,3,512]{2,1,0:T(4,128)S(1)} %copy.9.own_ref), channel_id=1, source_target_pairs={{1,0},{2,1},{3,2},{4,3},{5,4},{6,5},{7,6},{8,7},{9,8},{10,9},{11,1... | collective-permute-start | bytes 73736 | tf_op jit(solution)/shard_map/ppermute | solution.py:28
  9.9 3.6 %collective-permute-start = (f32[4,3,512]{2,1,0:T(4,128)S(1)}, f32[4,3,512]{2,1,0:T(4,128)S(1)}, u32[]{:S(2)}, u32[]{:S(2)}) collective-permute-start(f32[4,3,512]{2,1,0:T(4,128)S(1)} %copy.9.own_ref), channel_id=1, source_target_pairs={{0,1},{1,2},{2,3},{3,4},{4,5},{5,6},{6,7},{7,8},{8,9},{9,10},{10,1... | collective-permute-start | bytes 73736 | tf_op jit(solution)/shard_map/ppermute | solution.py:28
  13.6 19.9 %collective-permute-done.1.next_ref = f32[4,3,512]{2,1,0:T(4,128)S(1)} collective-permute-done((f32[4,3,512]{2,1,0:T(4,128)S(1)}, f32[4,3,512]{2,1,0:T(4,128)S(1)}, u32[]{:S(2)}, u32[]{:S(2)}) %collective-permute-start.1) | collective-permute-done | bytes 24608 | tf_op jit(solution)/shard_map/ppermute | solution.py:28
  33.5 0.0 collective-permute-done.prev_ref
  33.5 0.0 copy-start.3
  33.5 0.7 copy-done.3
  34.2 0.0 copy-start.5
  34.2 0.7 copy-done.5
  34.8 0.0 copy-start.6
  34.8 0.7 copy-done.6
  35.5 0.0 copy-start.7
  35.5 0.7 copy-done.7
  36.2 0.0 copy-start.4
  36.2 0.0 copy-start.2
  36.2 17.4 %blocks.1.k_ref = bf16[24,512,512]{2,1,0:T(8,128)(2,1)S(1)} custom-call(s32[24]{0:T(128)S(1)} %copy-done.7, s32[24]{0:T(128)S(1)} %copy-done.6, s32[24]{0:T(128)S(1)} %copy-done.5, s32[1]{0:T(128)} %bitcast.first_ref, s32[4,6]{1,0:T(4,128)S(1)} %copy-done.3, f32[4,3,512]{2,1,0:T(4,128)S(1)} %collective-permute-done.prev_ref, f32[4,3,512]{2,1,0:T(4,128)S(1)} %copy.9.own_ref, ...), custom_call_target="tpu_custom_call" | custom-call | tf_op jit(solution)/shard_map/blocks/pallas_call | solution.py:235
  53.6 0.0 copy-start
  53.6 4.5 %copy-done = bf16[24,512,512]{2,1,0:T(8,128)(2,1)} copy-done((bf16[24,512,512]{2,1,0:T(8,128)(2,1)}, bf16[24,512,512]{2,1,0:T(8,128)(2,1)S(1)}, u32[]{:S(2)}) %copy-start) | copy-done | bytes 12582936
  58.1 0.0 collective-permute-done.2.prev_ref
  58.1 0.0 collective-permute-done.3.next_ref
  58.2 0.0 copy-done.1
  58.2 0.0 copy-done.4
  58.2 8.8 %samples.1.s_ref = f32[4,512,256]{2,1,0:T(8,128)S(1)} custom-call(s32[1]{0:T(128)} %bitcast.first_ref, s32[4,6]{1,0:T(4,128)S(1)} %copy-done.4, bf16[24,512,512]{2,1,0:T(8,128)(2,1)} %copy-done, bf16[4,512,256]{2,1,0:T(8,128)(2,1)S(1)} %collective-permute-done.2.prev_ref, bf16[4,512,256]{2,1,0:T(8,128)(2,1)S(1)} %copy-done.1, ...), custom_call_target="tpu_custom_call" | custom-call | tf_op jit(solution)/shard_map/samples/pallas_call | solution.py:281
  66.9 0.0 copy-done.2
  66.9 23.1 %shard_map.86 = (bf16[4,512,256]{2,1,0:T(8,128)(2,1)}, f32[4,256,256]{2,1,0:T(8,128)}) custom-call(f32[4,512,256]{2,1,0:T(8,128)S(1)} %samples.1.s_ref, s32[4,512]{1,0:T(4,128)S(1)} %copy-done.2), custom_call_target="tpu_custom_call" | custom-call | tf_op jit(solution)/shard_map/pallas_call | solution.py:190
Async XLA Ops:
  0.6 57.5 %copy-start.1 = (bf16[4,512,256]{2,1,0:T(8,128)(2,1)S(1)}, bf16[4,512,256]{2,1,0:T(8,128)(2,1)}, u32[]{:S(2)}) copy-start(bf16[4,512,256]{2,1,0:T(8,128)(2,1)} %own_ref.2) | copy-start | bytes 3145732
  0.6 57.5 %collective-permute-start.2 = (bf16[4,512,256]{2,1,0:T(8,128)(2,1)}, bf16[4,512,256]{2,1,0:T(8,128)(2,1)S(1)}, u32[]{:S(2)}, u32[]{:S(2)}) collective-permute-start(bf16[4,512,256]{2,1,0:T(8,128)(2,1)} %own_ref.2), channel_id=1, source_target_pairs={{0,1},{1,2},{2,3},{3,4},{4,5},{5,6},{6,7},{7,8},{8,9},{9,10},{10,1... | collective-permute-start | bytes 3145736 | tf_op jit(solution)/shard_map/ppermute | solution.py:28
  5.3 52.9 %collective-permute-start.3 = (bf16[4,512,256]{2,1,0:T(8,128)(2,1)}, bf16[4,512,256]{2,1,0:T(8,128)(2,1)S(1)}, u32[]{:S(2)}, u32[]{:S(2)}) collective-permute-start(bf16[4,512,256]{2,1,0:T(8,128)(2,1)} %own_ref.2), channel_id=1, source_target_pairs={{1,0},{2,1},{3,2},{4,3},{5,4},{6,5},{7,6},{8,7},{9,8},{10,9},{11,1... | collective-permute-start | bytes 3145736 | tf_op jit(solution)/shard_map/ppermute | solution.py:28
  8.0 25.5 %collective-permute-start.1 = (f32[4,3,512]{2,1,0:T(4,128)S(1)}, f32[4,3,512]{2,1,0:T(4,128)S(1)}, u32[]{:S(2)}, u32[]{:S(2)}) collective-permute-start(f32[4,3,512]{2,1,0:T(4,128)S(1)} %copy.9.own_ref), channel_id=1, source_target_pairs={{1,0},{2,1},{3,2},{4,3},{5,4},{6,5},{7,6},{8,7},{9,8},{10,9},{11,1... | collective-permute-start | bytes 73736 | tf_op jit(solution)/shard_map/ppermute | solution.py:28
  9.9 23.6 %collective-permute-start = (f32[4,3,512]{2,1,0:T(4,128)S(1)}, f32[4,3,512]{2,1,0:T(4,128)S(1)}, u32[]{:S(2)}, u32[]{:S(2)}) collective-permute-start(f32[4,3,512]{2,1,0:T(4,128)S(1)} %copy.9.own_ref), channel_id=1, source_target_pairs={{0,1},{1,2},{2,3},{3,4},{4,5},{5,6},{6,7},{7,8},{8,9},{9,10},{10,1... | collective-permute-start | bytes 73736 | tf_op jit(solution)/shard_map/ppermute | solution.py:28
  33.5 0.7 copy-start.3
  34.2 0.7 copy-start.5
  34.8 0.7 copy-start.6
  35.5 0.7 copy-start.7
  36.2 22.0 %copy-start.4 = (s32[4,6]{1,0:T(4,128)S(1)}, s32[4,6]{1,0:T(4,128)}, u32[]{:S(2)}) copy-start(s32[4,6]{1,0:T(4,128)} %pattern_ref.3) | copy-start | bytes 292
  36.2 30.8 %copy-start.2 = (s32[4,512]{1,0:T(4,128)S(1)}, s32[4,512]{1,0:T(4,128)}, u32[]{:S(2)}) copy-start(s32[4,512]{1,0:T(4,128)} %order_ref.1) | copy-start | bytes 24580
  53.6 4.5 %copy-start = (bf16[24,512,512]{2,1,0:T(8,128)(2,1)}, bf16[24,512,512]{2,1,0:T(8,128)(2,1)S(1)}, u32[]{:S(2)}) copy-start(bf16[24,512,512]{2,1,0:T(8,128)(2,1)S(1)} %blocks.1.k_ref) | copy-start | bytes 37748740
where the time goes:
time: 91.6 us; the launch traced here: 90 us
  Pallas kernels  49.3 us (54%)
  waiting for transfers between devices  20 us (22%)
  starting transfers between devices  12.1 us (13%)
  local copies, waits for them, and re-layouts  7.93 us (9%)
    pallas_call x1, Pallas kernels, chol_call(): pl.pallas_call(functools.partial(chol_body, panel=panel, micro=micro), ou...  23.1 us
    ppermute x4, waiting for transfers between devices, passed_along(): return lax.ppermute(array, AXES, pairs)  20 us
    pallas_call x1, Pallas kernels, blocks_of(): pl.pallas_call(functools.partial(blocks_body, total=total), grid_spec=plt...  17.4 us
    ppermute x4, starting transfers between devices, passed_along(): return lax.ppermute(array, AXES, pairs)  12.1 us
    pallas_call x1, Pallas kernels, samples_of(): pl.pallas_call(functools.partial(samples_body, total=total, count=count,...  8.76 us
    unnamed x17, local copies, waits for them, and re-layouts  7.93 us
  transfers between devices with their start and end apart: 4, of which 1 were waited for; matrix products, arithmetic and copies ran while one was open for 1% of the time, Pallas kernels for 19%

commit v1 on v0

--- a/solution.py
+++ b/solution.py
@@ -1,7 +1,6 @@
 import functools
 import math
 
-import numpy as np
 import jax
 import jax.numpy as jnp
 from jax import lax
@@ -129,12 +128,23 @@
             rows[half, at, :] = x - tx
             rows[1 - half, at, :] = y - ty
 
-def chol_body(s_ref, order_ref, basis_ref, factor_ref, mat, inv_ref, rows, ups, *, panel, micro):
+def finish_body(k_ref, prev_ref, own_ref, next_ref, order_ref, basis_ref, factor_ref, s_ref, mat, inv_ref, rows, ups, *, panel, micro):
     count, points, width = s_ref.shape
     row_id = lax.broadcasted_iota(jnp.int32, (width, width), 0)
     col_id = lax.broadcasted_iota(jnp.int32, (width, width), 1)
+    refs = (prev_ref, own_ref, next_ref)
     for c in range(count):
-        hi, lo = halves(s_ref[c])
+        samples = None
+        for column, distance in enumerate(offset_table(W)):
+            slot = c + count + distance
+            term = jnp.dot(
+                k_ref[c, :, column * points:(column + 1) * points],
+                refs[slot // count][slot % count],
+                preferred_element_type=f32,
+            )
+            samples = term if samples is None else samples + term
+        s_ref[c] = samples
+        hi, lo = halves(samples)
         gram = contract(hi, hi, 0, 0)
         cross = contract(hi, lo, 0, 0)
         gram = gram + (cross + cross.T)
@@ -185,125 +195,92 @@
         pick = jnp.concatenate([jnp.where(order_t == place + f32(128 * q), f32(1), f32(0)).astype(bf16) for q in range(points // 128)], axis=1)
         basis_ref[c] = jnp.dot(pick, b, preferred_element_type=f32).astype(bf16)
 
-def chol_call(s, order, panel=64, micro=8, interpret=False):
-    count, points, width = s.shape
+def finish(blocks, prev, own, after, order, panel=64, micro=8):
+    count, points, width = own.shape
+    whole = pl.BlockSpec(memory_space=pltpu.VMEM)
     return pl.pallas_call(
-        functools.partial(chol_body, panel=panel, micro=micro),
-        out_shape=(jax.ShapeDtypeStruct((count, points, width), bf16), jax.ShapeDtypeStruct((count, width, width), f32)),
-        scratch_shapes=[pltpu.VMEM((count, width, width), f32), pltpu.VMEM((count, width, width), f32),
-            pltpu.VMEM((2, 8 * panel, 128), f32), pltpu.VMEM((8 * panel, 128), f32)],
-        compiler_params=pltpu.CompilerParams(vmem_limit_bytes=48 * 2**20),
-    )(s, order)
-
-
-def active(first, pattern, cluster, column, distance, total):
+        functools.partial(finish_body, panel=panel, micro=micro),
+        in_specs=[whole] * 5,
+        out_shape=(
+            jax.ShapeDtypeStruct((count, points, width), bf16),
+            jax.ShapeDtypeStruct((count, width, width), f32),
+        ),
+        scratch_shapes=[
+            pltpu.VMEM((count, points, width), f32),
+            pltpu.VMEM((count, width, width), f32),
+            pltpu.VMEM((count, width, width), f32),
+            pltpu.VMEM((2, 8 * panel, 128), f32),
+            pltpu.VMEM((8 * panel, 128), f32),
+        ],
+        compiler_params=pltpu.CompilerParams(vmem_limit_bytes=28 * 2**20),
+        name="finish",
+    )(*(pltpu.with_memory_space_constraint(x, pltpu.VMEM) for x in (blocks, prev, own, after)), order)
+
+
+def active(first, pattern, cluster, distance, total):
     source = first + cluster + distance
     return (pattern != 0) & (source >= 0) & (source < total)
 
 
-def blocks_body(cl_ref, co_ref, di_ref, first_ref, pattern_ref, prev_ref, own_ref, next_ref, out_ref, window, *, total):
-    step = pl.program_id(0)
-    count, _, points = own_ref.shape
-    first = first_ref[0]
-
-    @pl.when(step == 0)
+def blocks_body(pattern_ref, prev_ref, own_ref, next_ref, out_ref, window, *, total):
+    cluster, column = pl.program_id(0), pl.program_id(1)
+    count, points = own_ref.shape[1:]
+    first = lax.axis_index(AXES) * count
+
+    @pl.when((cluster == 0) & (column == 0))
     def _():
         window[...] = jnp.zeros_like(window)
         for slot in range(3 * count):
             ref = (prev_ref, own_ref, next_ref)[slot // count]
             index = (first + (slot - count)).astype(f32)
-            xs = ref[slot % count]
-            along = (xs[0:1] + index) - index
-            window[slot, 0:1, :] = along
-            window[slot, 1:3, :] = xs[1:3]
-
-    cluster = cl_ref[step]
-    column = co_ref[step]
-    distance = di_ref[step]
-
-    @pl.when(active(first, pattern_ref[cluster, column], cluster, column, distance, total))
+            at = slot % count
+            window[slot, 0:1, :] = (ref[0, at:at + 1, :] + index) - index
+            window[slot, 1:2, :] = ref[1, at:at + 1, :]
+            window[slot, 2:3, :] = ref[2, at:at + 1, :]
+
+    distance = column - W + jnp.where(column >= W - 1, 3, 0)
+    counted = active(first, pattern_ref[cluster, column], cluster, distance, total)
+
+    @pl.when(counted)
     def _():
         squares = turn_squares(window[count + cluster], window[count + cluster + distance], distance)
         out_ref[0] = kernel_values(squares, points).astype(bf16)
 
-
-def blocks_of(pairs, first, pattern, prev, own, after, total):
-    count, _, points = own.shape
-    table = offset_table(W)
-    tabs = [jnp.asarray(np.array(x, np.int32)) for x in zip(*[(c, k, table[k]) for c, k in pairs])]
+    @pl.when(jnp.logical_not(counted))
+    def _():
+        out_ref[...] = jnp.zeros_like(out_ref)
+
+
+def blocks_of(pattern, prev, own, after, total):
+    count, points = own.shape[1:]
+    columns = pattern.shape[1]
+    values = count * columns * points * points
     whole = pl.BlockSpec(memory_space=pltpu.VMEM)
     return pl.pallas_call(
         functools.partial(blocks_body, total=total),
-        grid_spec=pltpu.PrefetchScalarGridSpec(
-            num_scalar_prefetch=5,
-            grid=(len(pairs),),
-            in_specs=[whole, whole, whole],
-            out_specs=pl.BlockSpec((1, points, points), lambda i, *_: (i, 0, 0)),
-            scratch_shapes=[pltpu.VMEM((3 * count, 8, points), f32)],
-        ),
-        out_shape=jax.ShapeDtypeStruct((len(pairs), points, points), bf16),
-        compiler_params=pltpu.CompilerParams(vmem_limit_bytes=32 * 2**20),
+        grid=(count, columns),
+        in_specs=[pl.BlockSpec(memory_space=pltpu.SMEM), whole, whole, whole],
+        out_specs=pl.BlockSpec((1, points, points), lambda c, k: (c, 0, k)),
+        scratch_shapes=[pltpu.VMEM((3 * count, 8, points), f32)],
+        out_shape=pltpu.VMEM((count, points, columns * points), bf16),
+        cost_estimate=pl.CostEstimate(flops=40 * values, bytes_accessed=2 * values, transcendentals=3 * values),
+        compiler_params=pltpu.CompilerParams(vmem_limit_bytes=16 * 2**20),
         name="blocks",
-    )(*tabs, first, pattern, prev, own, after)
-
-
-def samples_body(first_ref, pattern_ref, k_ref, prev_ref, own_ref, next_ref, out_ref, *, total, count, table):
-    cluster = pl.program_id(0)
-    first = first_ref[0]
-    for column, distance in enumerate(table):
-        if column == 0:
-            out_ref[...] = jnp.zeros_like(out_ref)
-
-        @pl.when(active(first, pattern_ref[cluster, column], cluster, column, distance, total))
-        def _():
-            slot = cluster + distance
-
-            def add(ref, index):
-                out_ref[0] += jnp.dot(k_ref[column], ref[index], preferred_element_type=f32)
-
-            @pl.when(slot < 0)
-            def _():
-                add(prev_ref, slot + count)
-
-            @pl.when((slot >= 0) & (slot < count))
-            def _():
-                add(own_ref, slot)
-
-            @pl.when(slot >= count)
-            def _():
-                add(next_ref, slot - count)
-
-
-def samples_of(first, pattern, blocks, prev, own, after, total):
-    count, points, width = own.shape
-    table = offset_table(W)
-    whole = pl.BlockSpec(memory_space=pltpu.VMEM)
-    return pl.pallas_call(
-        functools.partial(samples_body, total=total, count=count, table=table),
-        grid_spec=pltpu.PrefetchScalarGridSpec(
-            num_scalar_prefetch=2,
-            grid=(count,),
-            in_specs=[pl.BlockSpec((len(table), points, points), lambda c, *_: (c, 0, 0)), whole, whole, whole],
-            out_specs=pl.BlockSpec((1, points, width), lambda c, *_: (c, 0, 0)),
-        ),
-        out_shape=jax.ShapeDtypeStruct((count, points, width), f32),
-        compiler_params=pltpu.CompilerParams(vmem_limit_bytes=40 * 2**20),
-        name="samples",
-    )(first, pattern, blocks, prev, own, after)
+    )(pattern, prev, own, after)
 
 
 def body(offsets, sketch, pattern, point_order):
     count = offsets.shape[0]
     total = count * lax.axis_size(AXES)
-    first = (lax.axis_index(AXES) * count).astype(jnp.int32).reshape(1)
+    offsets = offsets.transpose(1, 0, 2)
     prev_offsets = passed_along(offsets, 1)
     next_offsets = passed_along(offsets, -1)
-    prev_sketch = passed_along(sketch, 1)
-    next_sketch = passed_along(sketch, -1)
-    pairs = [(c, k) for c in range(count) for k in range(len(offset_table(W)))]
-    blocks = blocks_of(pairs, first, pattern, prev_offsets, offsets, next_offsets, total)
-    samples = samples_of(first, pattern, blocks, prev_sketch, sketch, next_sketch, total)
-    return chol_call(samples, point_order)
+    upward, prev_offsets = lax.optimization_barrier((sketch, prev_offsets))
+    downward, next_offsets = lax.optimization_barrier((sketch, next_offsets))
+    prev_sketch = passed_along(upward, 1)
+    next_sketch = passed_along(downward, -1)
+    blocks = blocks_of(pattern, prev_offsets, offsets, next_offsets, total)
+    return finish(blocks, prev_sketch, sketch, next_sketch, point_order)
 
 
 def solution(mesh):

time: 91.6 us -> 74.6 us (0.81)
  the two profiles are of different devices: /device:TPU:1 before, /device:TPU:4 now
where the time goes in v1:
time: 74.6 us; the launch traced here: 73.4 us
  Pallas kernels  47.2 us (63%)
  starting transfers between devices  17 us (23%)
  waiting for transfers between devices  7.02 us (9%)
  local copies, waits for them, and re-layouts  1.42 us (2%)
    pallas_call x1, Pallas kernels, finish(): pl.pallas_call(functools.partial(finish_body, panel=panel, micro=micro),...  28 us
    pallas_call x1, Pallas kernels, blocks_of(): pl.pallas_call(functools.partial(blocks_body, total=total), grid=(count,...  19.2 us
    ppermute x4, starting transfers between devices, passed_along(): return lax.ppermute(array, AXES, pairs)  17 us
    ppermute x4, waiting for transfers between devices, passed_along(): return lax.ppermute(array, AXES, pairs)  7.02 us
  transfers between devices with their start and end apart: 4, of which 1 were waited for; matrix products, arithmetic and copies ran while one was open for 0% of the time, Pallas kernels for 26%

profile of v1, /device:TPU:4, one launch (start us, length us, event | category | flops | bytes accessed | tf_op | source)
XLA Modules:
  0.0 73.4 jit_solution(17868162541703772295)
XLA Ops:
  0.6 0.0 copy-start
  0.6 0.0 copy-start.1
  0.7 6.0 %collective-permute-start.1 = (f32[3,4,512]{2,1,0:T(4,128)}, f32[3,4,512]{2,1,0:T(4,128)S(1)}, u32[]{:S(2)}, u32[]{:S(2)}) collective-permute-start(f32[3,4,512]{2,1,0:T(4,128)} %bitcast.1), channel_id=1, source_target_pairs={{1,0},{2,1},{3,2},{4,3},{5,4},{6,5},{7,6},{8,7},{9,8},{10,9},{11,1... | collective-permute-start | bytes 73736 | tf_op jit(solution)/shard_map/ppermute | solution.py:27
  6.6 1.9 %collective-permute-start = (f32[3,4,512]{2,1,0:T(4,128)}, f32[3,4,512]{2,1,0:T(4,128)S(1)}, u32[]{:S(2)}, u32[]{:S(2)}) collective-permute-start(f32[3,4,512]{2,1,0:T(4,128)} %bitcast.2), channel_id=1, source_target_pairs={{0,1},{1,2},{2,3},{3,4},{4,5},{5,6},{6,7},{7,8},{8,9},{9,10},{10,1... | collective-permute-start | bytes 73736 | tf_op jit(solution)/shard_map/ppermute | solution.py:27
  8.5 0.0 collective-permute-done.1.next_ref
  8.5 7.0 %collective-permute-done.prev_ref = f32[3,4,512]{2,1,0:T(4,128)S(1)} collective-permute-done((f32[3,4,512]{2,1,0:T(4,128)}, f32[3,4,512]{2,1,0:T(4,128)S(1)}, u32[]{:S(2)}, u32[]{:S(2)}) %collective-permute-start) | collective-permute-done | bytes 24608 | tf_op jit(solution)/shard_map/ppermute | solution.py:27
  15.6 1.9 %collective-permute-start.2 = (bf16[4,512,256]{2,1,0:T(8,128)(2,1)}, bf16[4,512,256]{2,1,0:T(8,128)(2,1)S(1)}, u32[]{:S(2)}, u32[]{:S(2)}) collective-permute-start(bf16[4,512,256]{2,1,0:T(8,128)(2,1)} %own_ref.1), channel_id=1, source_target_pairs={{0,1},{1,2},{2,3},{3,4},{4,5},{5,6},{6,7},{7,8},{8,9},{9,10},{10,1... | collective-permute-start | bytes 3145736 | tf_op jit(solution)/shard_map/ppermute | solution.py:27
  17.5 7.2 %collective-permute-start.3 = (bf16[4,512,256]{2,1,0:T(8,128)(2,1)}, bf16[4,512,256]{2,1,0:T(8,128)(2,1)S(1)}, u32[]{:S(2)}, u32[]{:S(2)}) collective-permute-start(bf16[4,512,256]{2,1,0:T(8,128)(2,1)} %own_ref.1), channel_id=1, source_target_pairs={{1,0},{2,1},{3,2},{4,3},{5,4},{6,5},{7,6},{8,7},{9,8},{10,9},{11,1... | collective-permute-start | bytes 3145736 | tf_op jit(solution)/shard_map/ppermute | solution.py:27
  24.7 0.0 copy-start.2
  24.7 0.7 copy-done.2
  25.5 0.0 copy-start.3
  25.5 0.7 copy-done.3
  26.1 19.2 %blocks.1.k_ref = bf16[4,512,3072]{2,1,0:T(8,128)(2,1)S(1)} custom-call(s32[4,6]{1,0:T(4,128)S(1)} %copy-done.3, f32[3,4,512]{2,1,0:T(4,128)S(1)} %collective-permute-done.prev_ref, f32[3,4,512]{2,1,0:T(4,128)S(1)} %bitcast.3, f32[3,4,512]{2,1,0:T(4,128)S(1)} %collective-permute-done.1.next_ref), custom_call_target="tpu_custom_call" | custom-call | flops 251658240 | bytes 12582912 | tf_op jit(solution)/shard_map/blocks/pallas_call | solution.py:259
  45.3 0.0 collective-permute-done.2.prev_ref
  45.3 0.0 collective-permute-done.3.next_ref
  45.3 0.0 copy-done
  45.4 0.0 copy-done.1
  45.4 28.0 %finish.1 = (bf16[4,512,256]{2,1,0:T(8,128)(2,1)}, f32[4,256,256]{2,1,0:T(8,128)}) custom-call(bf16[4,512,3072]{2,1,0:T(8,128)(2,1)S(1)} %blocks.1.k_ref, bf16[4,512,256]{2,1,0:T(8,128)(2,1)S(1)} %collective-permute-done.2.prev_ref, bf16[4,512,256]{2,1,0:T(8,128)(2,1)S(1)} %copy-done, bf16[4,512,256]{2,1,0:T(8,128)(2,1)S(1)} %collective-permute-done.3.next_ref, ...), custom_call_target="tpu_custom_call" | custom-call | tf_op jit(solution)/shard_map/finish/pallas_call | solution.py:201
Async XLA Ops:
  0.6 44.7 %copy-start = (bf16[4,512,256]{2,1,0:T(8,128)(2,1)S(1)}, bf16[4,512,256]{2,1,0:T(8,128)(2,1)}, u32[]{:S(2)}) copy-start(bf16[4,512,256]{2,1,0:T(8,128)(2,1)} %own_ref.1) | copy-start | bytes 3145732
  0.6 44.7 %copy-start.1 = (s32[4,512]{1,0:T(4,128)S(1)}, s32[4,512]{1,0:T(4,128)}, u32[]{:S(2)}) copy-start(s32[4,512]{1,0:T(4,128)} %order_ref.1) | copy-start | bytes 24580
  0.7 7.9 %collective-permute-start.1 = (f32[3,4,512]{2,1,0:T(4,128)}, f32[3,4,512]{2,1,0:T(4,128)S(1)}, u32[]{:S(2)}, u32[]{:S(2)}) collective-permute-start(f32[3,4,512]{2,1,0:T(4,128)} %bitcast.1), channel_id=1, source_target_pairs={{1,0},{2,1},{3,2},{4,3},{5,4},{6,5},{7,6},{8,7},{9,8},{10,9},{11,1... | collective-permute-start | bytes 73736 | tf_op jit(solution)/shard_map/ppermute | solution.py:27
  6.6 9.0 %collective-permute-start = (f32[3,4,512]{2,1,0:T(4,128)}, f32[3,4,512]{2,1,0:T(4,128)S(1)}, u32[]{:S(2)}, u32[]{:S(2)}) collective-permute-start(f32[3,4,512]{2,1,0:T(4,128)} %bitcast.2), channel_id=1, source_target_pairs={{0,1},{1,2},{2,3},{3,4},{4,5},{5,6},{6,7},{7,8},{8,9},{9,10},{10,1... | collective-permute-start | bytes 73736 | tf_op jit(solution)/shard_map/ppermute | solution.py:27
  15.6 29.8 %collective-permute-start.2 = (bf16[4,512,256]{2,1,0:T(8,128)(2,1)}, bf16[4,512,256]{2,1,0:T(8,128)(2,1)S(1)}, u32[]{:S(2)}, u32[]{:S(2)}) collective-permute-start(bf16[4,512,256]{2,1,0:T(8,128)(2,1)} %own_ref.1), channel_id=1, source_target_pairs={{0,1},{1,2},{2,3},{3,4},{4,5},{5,6},{6,7},{7,8},{8,9},{9,10},{10,1... | collective-permute-start | bytes 3145736 | tf_op jit(solution)/shard_map/ppermute | solution.py:27
  17.5 27.9 %collective-permute-start.3 = (bf16[4,512,256]{2,1,0:T(8,128)(2,1)}, bf16[4,512,256]{2,1,0:T(8,128)(2,1)S(1)}, u32[]{:S(2)}, u32[]{:S(2)}) collective-permute-start(bf16[4,512,256]{2,1,0:T(8,128)(2,1)} %own_ref.1), channel_id=1, source_target_pairs={{1,0},{2,1},{3,2},{4,3},{5,4},{6,5},{7,6},{8,7},{9,8},{10,9},{11,1... | collective-permute-start | bytes 3145736 | tf_op jit(solution)/shard_map/ppermute | solution.py:27
  24.7 0.7 %copy-start.2 = (f32[4,3,512]{2,0,1:T(4,128)S(1)}, f32[4,3,512]{2,0,1:T(4,128)}, u32[]{:S(2)}) copy-start(f32[4,3,512]{2,0,1:T(4,128)} %param.4) | copy-start | bytes 73732
  25.5 0.7 copy-start.3

commit v2 on v1

--- a/solution.py
+++ b/solution.py
@@ -21,10 +21,10 @@
 SINE = (4.44288292, -7.30824569, 3.60635423, -0.84611167, 0.10982452)
 
 
-def passed_along(array, by):
+def exchanged(array, start):
     peers = lax.axis_size(AXES)
-    pairs = [(i, i + by) for i in range(peers) if 0 <= i + by < peers]
-    return lax.ppermute(array, AXES, pairs)
+    pairs = [(i, i + 1) for i in range(start, peers - 1, 2)]
+    return lax.ppermute(array, AXES, pairs + [(j, i) for i, j in pairs])
 
 
 def offset_table(reach):
@@ -128,22 +128,29 @@
             rows[half, at, :] = x - tx
             rows[1 - half, at, :] = y - ty
 
-def finish_body(k_ref, prev_ref, own_ref, next_ref, order_ref, basis_ref, factor_ref, s_ref, mat, inv_ref, rows, ups, *, panel, micro):
+def finish_body(k_ref, even_ref, own_ref, odd_ref, order_ref, basis_ref, factor_ref, s_ref, mat, inv_ref, rows, ups, *, panel, micro):
     count, points, width = s_ref.shape
     row_id = lax.broadcasted_iota(jnp.int32, (width, width), 0)
     col_id = lax.broadcasted_iota(jnp.int32, (width, width), 1)
-    refs = (prev_ref, own_ref, next_ref)
+
+    def fill(refs):
+        for c in range(count):
+            samples = None
+            for column, distance in enumerate(offset_table(W)):
+                slot = c + count + distance
+                term = jnp.dot(
+                    k_ref[c, :, column * points:(column + 1) * points],
+                    refs[slot // count][slot % count],
+                    preferred_element_type=f32,
+                )
+                samples = term if samples is None else samples + term
+            s_ref[c] = samples
+
+    side = lax.rem(lax.axis_index(AXES), 2)
+    pl.when(side == 1)(lambda: fill((even_ref, own_ref, odd_ref)))
+    pl.when(side == 0)(lambda: fill((odd_ref, own_ref, even_ref)))
     for c in range(count):
-        samples = None
-        for column, distance in enumerate(offset_table(W)):
-            slot = c + count + distance
-            term = jnp.dot(
-                k_ref[c, :, column * points:(column + 1) * points],
-                refs[slot // count][slot % count],
-                preferred_element_type=f32,
-            )
-            samples = term if samples is None else samples + term
-        s_ref[c] = samples
+        samples = s_ref[c]
         hi, lo = halves(samples)
         gram = contract(hi, hi, 0, 0)
         cross = contract(hi, lo, 0, 0)
@@ -195,7 +202,7 @@
         pick = jnp.concatenate([jnp.where(order_t == place + f32(128 * q), f32(1), f32(0)).astype(bf16) for q in range(points // 128)], axis=1)
         basis_ref[c] = jnp.dot(pick, b, preferred_element_type=f32).astype(bf16)
 
-def finish(blocks, prev, own, after, order, panel=64, micro=8):
+def finish(blocks, even, own, odd, order, panel=64, micro=8):
     count, points, width = own.shape
     whole = pl.BlockSpec(memory_space=pltpu.VMEM)
     return pl.pallas_call(
@@ -214,7 +221,7 @@
         ],
         compiler_params=pltpu.CompilerParams(vmem_limit_bytes=28 * 2**20),
         name="finish",
-    )(*(pltpu.with_memory_space_constraint(x, pltpu.VMEM) for x in (blocks, prev, own, after)), order)
+    )(*(pltpu.with_memory_space_constraint(x, pltpu.VMEM) for x in (blocks, even, own, odd)), order)
 
 
 def active(first, pattern, cluster, distance, total):
@@ -222,21 +229,23 @@
     return (pattern != 0) & (source >= 0) & (source < total)
 
 
-def blocks_body(pattern_ref, prev_ref, own_ref, next_ref, out_ref, window, *, total):
+def blocks_body(pattern_ref, even_ref, own_ref, odd_ref, out_ref, window, *, total):
     cluster, column = pl.program_id(0), pl.program_id(1)
     count, points = own_ref.shape[1:]
-    first = lax.axis_index(AXES) * count
+    me = lax.axis_index(AXES)
+    first = me * count
+    side = lax.rem(me, 2)
 
     @pl.when((cluster == 0) & (column == 0))
     def _():
         window[...] = jnp.zeros_like(window)
-        for slot in range(3 * count):
-            ref = (prev_ref, own_ref, next_ref)[slot // count]
-            index = (first + (slot - count)).astype(f32)
-            at = slot % count
-            window[slot, 0:1, :] = (ref[0, at:at + 1, :] + index) - index
-            window[slot, 1:2, :] = ref[1, at:at + 1, :]
-            window[slot, 2:3, :] = ref[2, at:at + 1, :]
+        for group, ref in ((2 - 2 * side, even_ref), (1, own_ref), (2 * side, odd_ref)):
+            for at in range(count):
+                slot = group * count + at
+                index = (first + (slot - count)).astype(f32)
+                window[slot, 0:1, :] = (ref[0, at:at + 1, :] + index) - index
+                window[slot, 1:2, :] = ref[1, at:at + 1, :]
+                window[slot, 2:3, :] = ref[2, at:at + 1, :]
 
     distance = column - W + jnp.where(column >= W - 1, 3, 0)
     counted = active(first, pattern_ref[cluster, column], cluster, distance, total)
@@ -251,7 +260,7 @@
         out_ref[...] = jnp.zeros_like(out_ref)
 
 
-def blocks_of(pattern, prev, own, after, total):
+def blocks_of(pattern, even, own, odd, total):
     count, points = own.shape[1:]
     columns = pattern.shape[1]
     values = count * columns * points * points
@@ -266,21 +275,20 @@
         cost_estimate=pl.CostEstimate(flops=40 * values, bytes_accessed=2 * values, transcendentals=3 * values),
         compiler_params=pltpu.CompilerParams(vmem_limit_bytes=16 * 2**20),
         name="blocks",
-    )(pattern, prev, own, after)
+    )(pattern, even, own, odd)
 
 
 def body(offsets, sketch, pattern, point_order):
     count = offsets.shape[0]
     total = count * lax.axis_size(AXES)
     offsets = offsets.transpose(1, 0, 2)
-    prev_offsets = passed_along(offsets, 1)
-    next_offsets = passed_along(offsets, -1)
-    upward, prev_offsets = lax.optimization_barrier((sketch, prev_offsets))
-    downward, next_offsets = lax.optimization_barrier((sketch, next_offsets))
-    prev_sketch = passed_along(upward, 1)
-    next_sketch = passed_along(downward, -1)
-    blocks = blocks_of(pattern, prev_offsets, offsets, next_offsets, total)
-    return finish(blocks, prev_sketch, sketch, next_sketch, point_order)
+    odd_offsets = exchanged(offsets, 1)
+    sent, odd_offsets = lax.optimization_barrier((sketch, odd_offsets))
+    odd_sketch = exchanged(sent, 1)
+    even_offsets = exchanged(offsets, 0)
+    even_sketch = exchanged(sketch, 0)
+    blocks = blocks_of(pattern, even_offsets, offsets, odd_offsets, total)
+    return finish(blocks, even_sketch, sketch, odd_sketch, point_order)
 
 
 def solution(mesh):

time: 74.6 us -> 66.9 us (0.90)
  the two profiles are of different devices: /device:TPU:4 before, /device:TPU:5 now
where the time goes in v2:
time: 66.9 us; the launch traced here: 67.7 us
  Pallas kernels  48.8 us (73%)
  starting transfers between devices  15.6 us (23%)
  local copies, waits for them, and re-layouts  1.43 us (2%)
  waiting for transfers between devices  1.07 us (2%)
  between operations  0.71 us (1%)
    pallas_call x1, Pallas kernels, finish(): pl.pallas_call(functools.partial(finish_body, panel=panel, micro=micro),...  26.7 us
    pallas_call x1, Pallas kernels, blocks_of(): pl.pallas_call(functools.partial(blocks_body, total=total), grid=(count,...  22.1 us
    ppermute x4, starting transfers between devices, exchanged(): return lax.ppermute(array, AXES, pairs + [(j, i) for i, j in pairs])  15.6 us
    unnamed x8, local copies, waits for them, and re-layouts  1.43 us
  transfers between devices with their start and end apart: 4, of which 1 were waited for; matrix products, arithmetic and copies ran while one was open for 0% of the time, Pallas kernels for 33%

profile of v2, /device:TPU:5, one launch (start us, length us, event | category | flops | bytes accessed | tf_op | source)
XLA Modules:
  0.0 67.7 jit_solution(5269884774970158675)
XLA Ops:
  0.6 0.0 copy-start
  0.6 0.0 copy-start.1
  0.7 3.8 %collective-permute-start.1 = (f32[3,4,512]{2,1,0:T(4,128)}, f32[3,4,512]{2,1,0:T(4,128)S(1)}, u32[]{:S(2)}, u32[]{:S(2)}) collective-permute-start(f32[3,4,512]{2,1,0:T(4,128)} %bitcast.1), channel_id=1, source_target_pairs={{1,2},{3,4},{5,6},{7,8},{9,10},{11,12},{13,14},{15,16},{17,18},{19... | collective-permute-start | bytes 73736 | tf_op jit(solution)/shard_map/ppermute | solution.py:27
  4.5 2.9 %collective-permute-start.2 = (bf16[4,512,256]{2,1,0:T(8,128)(2,1)}, bf16[4,512,256]{2,1,0:T(8,128)(2,1)S(1)}, u32[]{:S(2)}, u32[]{:S(2)}) collective-permute-start(bf16[4,512,256]{2,1,0:T(8,128)(2,1)} %own_ref.1), channel_id=1, source_target_pairs={{0,1},{2,3},{4,5},{6,7},{8,9},{10,11},{12,13},{14,15},{16,17},{18,... | collective-permute-start | bytes 3145736 | tf_op jit(solution)/shard_map/ppermute | solution.py:27
  7.3 0.0 collective-permute-done.1.odd_ref
  7.4 2.5 %collective-permute-start.3 = (bf16[4,512,256]{2,1,0:T(8,128)(2,1)}, bf16[4,512,256]{2,1,0:T(8,128)(2,1)S(1)}, u32[]{:S(2)}, u32[]{:S(2)}) collective-permute-start(bf16[4,512,256]{2,1,0:T(8,128)(2,1)} %own_ref.1), channel_id=1, source_target_pairs={{1,2},{3,4},{5,6},{7,8},{9,10},{11,12},{13,14},{15,16},{17,18},{19... | collective-permute-start | bytes 3145736 | tf_op jit(solution)/shard_map/ppermute | solution.py:27
  9.8 6.5 %collective-permute-start = (f32[3,4,512]{2,1,0:T(4,128)}, f32[3,4,512]{2,1,0:T(4,128)S(1)}, u32[]{:S(2)}, u32[]{:S(2)}) collective-permute-start(f32[3,4,512]{2,1,0:T(4,128)} %bitcast.2), channel_id=1, source_target_pairs={{0,1},{2,3},{4,5},{6,7},{8,9},{10,11},{12,13},{14,15},{16,17},{18,... | collective-permute-start | bytes 73736 | tf_op jit(solution)/shard_map/ppermute | solution.py:27
  16.3 1.1 %collective-permute-done.even_ref = f32[3,4,512]{2,1,0:T(4,128)S(1)} collective-permute-done((f32[3,4,512]{2,1,0:T(4,128)}, f32[3,4,512]{2,1,0:T(4,128)S(1)}, u32[]{:S(2)}, u32[]{:S(2)}) %collective-permute-start) | collective-permute-done | bytes 24608 | tf_op jit(solution)/shard_map/ppermute | solution.py:27
  17.4 0.0 copy-start.2
  17.4 0.7 %copy-done.2 = f32[4,3,512]{2,0,1:T(4,128)S(1)} copy-done((f32[4,3,512]{2,0,1:T(4,128)S(1)}, f32[4,3,512]{2,0,1:T(4,128)}, u32[]{:S(2)}) %copy-start.2) | copy-done | bytes 24600
  18.1 0.0 copy-start.3
  18.1 0.7 %copy-done.3 = s32[4,6]{1,0:T(4,128)S(1)} copy-done((s32[4,6]{1,0:T(4,128)S(1)}, s32[4,6]{1,0:T(4,128)}, u32[]{:S(2)}) %copy-start.3) | copy-done | bytes 120
  18.8 22.1 %blocks.1.k_ref = bf16[4,512,3072]{2,1,0:T(8,128)(2,1)S(1)} custom-call(s32[4,6]{1,0:T(4,128)S(1)} %copy-done.3, f32[3,4,512]{2,1,0:T(4,128)S(1)} %collective-permute-done.even_ref, f32[3,4,512]{2,1,0:T(4,128)S(1)} %bitcast.3, f32[3,4,512]{2,1,0:T(4,128)S(1)} %collective-permute-done.1.odd_ref), custom_call_target="tpu_custom_call" | custom-call | flops 251658240 | bytes 12582912 | tf_op jit(solution)/shard_map/blocks/pallas_call | solution.py:268
  40.9 0.0 collective-permute-done.2.even_ref
  40.9 0.0 collective-permute-done.3.odd_ref
  40.9 0.0 copy-done
  41.0 0.0 copy-done.1
  41.0 26.7 %finish.1 = (bf16[4,512,256]{2,1,0:T(8,128)(2,1)}, f32[4,256,256]{2,1,0:T(8,128)}) custom-call(bf16[4,512,3072]{2,1,0:T(8,128)(2,1)S(1)} %blocks.1.k_ref, bf16[4,512,256]{2,1,0:T(8,128)(2,1)S(1)} %collective-permute-done.2.even_ref, bf16[4,512,256]{2,1,0:T(8,128)(2,1)S(1)} %copy-done, bf16[4,512,256]{2,1,0:T(8,128)(2,1)S(1)} %collective-permute-done.3.odd_ref, ...), custom_call_target="tpu_custom_call" | custom-call | tf_op jit(solution)/shard_map/finish/pallas_call | solution.py:208
Async XLA Ops:
  0.6 40.3 %copy-start = (bf16[4,512,256]{2,1,0:T(8,128)(2,1)S(1)}, bf16[4,512,256]{2,1,0:T(8,128)(2,1)}, u32[]{:S(2)}) copy-start(bf16[4,512,256]{2,1,0:T(8,128)(2,1)} %own_ref.1) | copy-start | bytes 3145732
  0.6 40.3 %copy-start.1 = (s32[4,512]{1,0:T(4,128)S(1)}, s32[4,512]{1,0:T(4,128)}, u32[]{:S(2)}) copy-start(s32[4,512]{1,0:T(4,128)} %order_ref.1) | copy-start | bytes 24580
  0.7 6.7 %collective-permute-start.1 = (f32[3,4,512]{2,1,0:T(4,128)}, f32[3,4,512]{2,1,0:T(4,128)S(1)}, u32[]{:S(2)}, u32[]{:S(2)}) collective-permute-start(f32[3,4,512]{2,1,0:T(4,128)} %bitcast.1), channel_id=1, source_target_pairs={{1,2},{3,4},{5,6},{7,8},{9,10},{11,12},{13,14},{15,16},{17,18},{19... | collective-permute-start | bytes 73736 | tf_op jit(solution)/shard_map/ppermute | solution.py:27
  4.5 36.5 %collective-permute-start.2 = (bf16[4,512,256]{2,1,0:T(8,128)(2,1)}, bf16[4,512,256]{2,1,0:T(8,128)(2,1)S(1)}, u32[]{:S(2)}, u32[]{:S(2)}) collective-permute-start(bf16[4,512,256]{2,1,0:T(8,128)(2,1)} %own_ref.1), channel_id=1, source_target_pairs={{0,1},{2,3},{4,5},{6,7},{8,9},{10,11},{12,13},{14,15},{16,17},{18,... | collective-permute-start | bytes 3145736 | tf_op jit(solution)/shard_map/ppermute | solution.py:27
  7.4 33.6 %collective-permute-start.3 = (bf16[4,512,256]{2,1,0:T(8,128)(2,1)}, bf16[4,512,256]{2,1,0:T(8,128)(2,1)S(1)}, u32[]{:S(2)}, u32[]{:S(2)}) collective-permute-start(bf16[4,512,256]{2,1,0:T(8,128)(2,1)} %own_ref.1), channel_id=1, source_target_pairs={{1,2},{3,4},{5,6},{7,8},{9,10},{11,12},{13,14},{15,16},{17,18},{19... | collective-permute-start | bytes 3145736 | tf_op jit(solution)/shard_map/ppermute | solution.py:27
  9.8 7.5 %collective-permute-start = (f32[3,4,512]{2,1,0:T(4,128)}, f32[3,4,512]{2,1,0:T(4,128)S(1)}, u32[]{:S(2)}, u32[]{:S(2)}) collective-permute-start(f32[3,4,512]{2,1,0:T(4,128)} %bitcast.2), channel_id=1, source_target_pairs={{0,1},{2,3},{4,5},{6,7},{8,9},{10,11},{12,13},{14,15},{16,17},{18,... | collective-permute-start | bytes 73736 | tf_op jit(solution)/shard_map/ppermute | solution.py:27
  17.4 0.7 %copy-start.2 = (f32[4,3,512]{2,0,1:T(4,128)S(1)}, f32[4,3,512]{2,0,1:T(4,128)}, u32[]{:S(2)}) copy-start(f32[4,3,512]{2,0,1:T(4,128)} %param.4) | copy-start | bytes 73732
  18.1 0.7 %copy-start.3 = (s32[4,6]{1,0:T(4,128)S(1)}, s32[4,6]{1,0:T(4,128)}, u32[]{:S(2)}) copy-start(s32[4,6]{1,0:T(4,128)} %pattern_ref.1) | copy-start | bytes 292

commit v3 on v2

--- a/solution.py
+++ b/solution.py
@@ -53,7 +53,7 @@
     return high, middle, low
 
 
-def turn_squares(target, source, distance):
+def split_points(target, source, distance):
     row = lax.broadcasted_iota(jnp.int32, target.shape, 0)
     half = distance.astype(f32) * f32(0.5)
 
@@ -70,7 +70,7 @@
     rh, rm, rl = pieces(right)
     a = jnp.concatenate([lh, lh, lm, lm, lh, ll, lm, ll], axis=0).astype(bf16)
     b = jnp.concatenate([rh, rm, rh, rm, rl, rh, rl, rm], axis=0).astype(bf16)
-    return contract(a, b, 0, 0)
+    return a, b
 
 
 def halves(x):
@@ -128,8 +128,8 @@
             rows[half, at, :] = x - tx
             rows[1 - half, at, :] = y - ty
 
-def finish_body(k_ref, even_ref, own_ref, odd_ref, order_ref, basis_ref, factor_ref, s_ref, mat, inv_ref, rows, ups, *, panel, micro):
-    count, points, width = s_ref.shape
+def finish_body(k_ref, even_ref, own_ref, odd_ref, order_ref, basis_ref, factor_ref, t_ref, mat, inv_ref, rows, ups, *, panel, micro):
+    count, width, points = own_ref.shape
     row_id = lax.broadcasted_iota(jnp.int32, (width, width), 0)
     col_id = lax.broadcasted_iota(jnp.int32, (width, width), 1)
 
@@ -138,23 +138,17 @@
             samples = None
             for column, distance in enumerate(offset_table(W)):
                 slot = c + count + distance
-                term = jnp.dot(
-                    k_ref[c, :, column * points:(column + 1) * points],
-                    refs[slot // count][slot % count],
-                    preferred_element_type=f32,
-                )
+                block = k_ref[len(offset_table(W)) * c + column]
+                term = jnp.dot(refs[slot // count][slot % count], block, preferred_element_type=f32)
                 samples = term if samples is None else samples + term
-            s_ref[c] = samples
+            t_ref[c] = samples
 
     side = lax.rem(lax.axis_index(AXES), 2)
     pl.when(side == 1)(lambda: fill((even_ref, own_ref, odd_ref)))
     pl.when(side == 0)(lambda: fill((odd_ref, own_ref, even_ref)))
     for c in range(count):
-        samples = s_ref[c]
-        hi, lo = halves(samples)
-        gram = contract(hi, hi, 0, 0)
-        cross = contract(hi, lo, 0, 0)
-        gram = gram + (cross + cross.T)
+        hi, lo = halves(t_ref[c])
+        gram = contract(jnp.concatenate([hi, hi, lo], axis=1), jnp.concatenate([hi, lo, hi], axis=1), 1, 1)
         shift = f32(0.01) * jnp.sum(jnp.where(row_id == col_id, gram, f32(0))) / f32(width) + f32(1e-5)
         mat[c] = gram + jnp.where(row_id == col_id, shift, f32(0))
     for first in range(0, width, panel):
@@ -192,18 +186,16 @@
                 old = jnp.where((cc >= first) & (cc < rest), f32(0), old)
                 mat[c, rest:, :] = old - prod
     for c in range(count):
-        hi, lo = halves(s_ref[c])
+        hi, lo = halves(t_ref[c])
         wh, wl = halves(inv_ref[c])
-        b = contract(jnp.concatenate([hi, hi, lo], axis=1), jnp.concatenate([wh, wl, wh], axis=1), 1, 1)
-        b = b.astype(bf16)
-        order = order_ref[c:c + 1, :].astype(f32)
-        order_t = jnp.broadcast_to(order, (128, points)).T
+        b = jnp.dot(jnp.concatenate([wh, wh, wl], axis=1), jnp.concatenate([hi, lo, hi], axis=0), preferred_element_type=f32).astype(bf16)
+        order_t = jnp.broadcast_to(order_ref[c:c + 1, :].astype(f32), (128, points)).T
         place = lax.broadcasted_iota(jnp.int32, (points, 128), 1).astype(f32)
         pick = jnp.concatenate([jnp.where(order_t == place + f32(128 * q), f32(1), f32(0)).astype(bf16) for q in range(points // 128)], axis=1)
-        basis_ref[c] = jnp.dot(pick, b, preferred_element_type=f32).astype(bf16)
-
-def finish(blocks, even, own, odd, order, panel=64, micro=8):
-    count, points, width = own.shape
+        basis_ref[c] = contract(pick, b, 1, 1).astype(bf16)
+
+def finish(blocks, even, own, odd, order, panel=16, micro=8):
+    count, width, points = own.shape
     whole = pl.BlockSpec(memory_space=pltpu.VMEM)
     return pl.pallas_call(
         functools.partial(finish_body, panel=panel, micro=micro),
@@ -213,7 +205,7 @@
             jax.ShapeDtypeStruct((count, width, width), f32),
         ),
         scratch_shapes=[
-            pltpu.VMEM((count, points, width), f32),
+            pltpu.VMEM((count, width, points), f32),
             pltpu.VMEM((count, width, width), f32),
             pltpu.VMEM((count, width, width), f32),
             pltpu.VMEM((2, 8 * panel, 128), f32),
@@ -224,54 +216,72 @@
     )(*(pltpu.with_memory_space_constraint(x, pltpu.VMEM) for x in (blocks, even, own, odd)), order)
 
 
-def active(first, pattern, cluster, distance, total):
-    source = first + cluster + distance
-    return (pattern != 0) & (source >= 0) & (source < total)
-
-
-def blocks_body(pattern_ref, even_ref, own_ref, odd_ref, out_ref, window, *, total):
-    cluster, column = pl.program_id(0), pl.program_id(1)
+def blocks_body(pattern_ref, even_ref, own_ref, odd_ref, out_ref, window, squares, listed, *, total):
     count, points = own_ref.shape[1:]
+    columns = pattern_ref.shape[1]
     me = lax.axis_index(AXES)
     first = me * count
     side = lax.rem(me, 2)
-
-    @pl.when((cluster == 0) & (column == 0))
-    def _():
-        window[...] = jnp.zeros_like(window)
-        for group, ref in ((2 - 2 * side, even_ref), (1, own_ref), (2 * side, odd_ref)):
-            for at in range(count):
-                slot = group * count + at
-                index = (first + (slot - count)).astype(f32)
-                window[slot, 0:1, :] = (ref[0, at:at + 1, :] + index) - index
-                window[slot, 1:2, :] = ref[1, at:at + 1, :]
-                window[slot, 2:3, :] = ref[2, at:at + 1, :]
-
-    distance = column - W + jnp.where(column >= W - 1, 3, 0)
-    counted = active(first, pattern_ref[cluster, column], cluster, distance, total)
-
-    @pl.when(counted)
-    def _():
-        squares = turn_squares(window[count + cluster], window[count + cluster + distance], distance)
-        out_ref[0] = kernel_values(squares, points).astype(bf16)
-
-    @pl.when(jnp.logical_not(counted))
-    def _():
-        out_ref[...] = jnp.zeros_like(out_ref)
+    window[...] = jnp.zeros_like(window)
+    for group, ref in ((2 - 2 * side, even_ref), (1, own_ref), (2 * side, odd_ref)):
+        for at in range(count):
+            slot = group * count + at
+            index = (first + (slot - count)).astype(f32)
+            window[slot, 0:1, :] = (ref[0, at:at + 1, :] + index) - index
+            window[slot, 1:2, :] = ref[1, at:at + 1, :]
+            window[slot, 2:3, :] = ref[2, at:at + 1, :]
+
+    def reach(column):
+        return column - W + jnp.where(column >= W - 1, 3, 0)
+
+    def note(pair, found):
+        cluster, column = pair // columns, lax.rem(pair, columns)
+        source = first + cluster + reach(column)
+        counted = (pattern_ref[cluster, column] != 0) & (source >= 0) & (source < total)
+        listed[found] = pair
+
+        @pl.when(jnp.logical_not(counted))
+        def _():
+            out_ref[pair] = jnp.zeros_like(out_ref[pair])
+
+        return found + counted.astype(jnp.int32)
+
+    found = lax.fori_loop(0, count * columns, note, jnp.int32(0))
+
+    def measure(step):
+        pair = listed[jnp.minimum(step, jnp.maximum(found - 1, 0))]
+        cluster, column = pair // columns, lax.rem(pair, columns)
+        distance = reach(column)
+        a, b = split_points(window[count + cluster], window[count + cluster + distance], distance)
+        return contract(b, a, 0, 0)
+
+    squares[0] = measure(jnp.int32(0))
+
+    def step(at, carry):
+        after = measure(at + 1)
+        out_ref[listed[at]] = kernel_values(squares[lax.rem(at, 2)], points).astype(bf16)
+        squares[lax.rem(at + 1, 2)] = after
+        return carry
+
+    lax.fori_loop(0, found, step, 0)
 
 
 def blocks_of(pattern, even, own, odd, total):
     count, points = own.shape[1:]
     columns = pattern.shape[1]
-    values = count * columns * points * points
+    pairs = count * columns
+    values = pairs * points * points
     whole = pl.BlockSpec(memory_space=pltpu.VMEM)
     return pl.pallas_call(
         functools.partial(blocks_body, total=total),
-        grid=(count, columns),
         in_specs=[pl.BlockSpec(memory_space=pltpu.SMEM), whole, whole, whole],
-        out_specs=pl.BlockSpec((1, points, points), lambda c, k: (c, 0, k)),
-        scratch_shapes=[pltpu.VMEM((3 * count, 8, points), f32)],
-        out_shape=pltpu.VMEM((count, points, columns * points), bf16),
+        out_specs=whole,
+        scratch_shapes=[
+            pltpu.VMEM((3 * count, 8, points), f32),
+            pltpu.VMEM((2, points, points), f32),
+            pltpu.SMEM((pairs + 1,), jnp.int32),
+        ],
+        out_shape=pltpu.VMEM((pairs, points, points), bf16),
         cost_estimate=pl.CostEstimate(flops=40 * values, bytes_accessed=2 * values, transcendentals=3 * values),
         compiler_params=pltpu.CompilerParams(vmem_limit_bytes=16 * 2**20),
         name="blocks",
@@ -283,12 +293,13 @@
     total = count * lax.axis_size(AXES)
     offsets = offsets.transpose(1, 0, 2)
     odd_offsets = exchanged(offsets, 1)
-    sent, odd_offsets = lax.optimization_barrier((sketch, odd_offsets))
+    turned = sketch.transpose(0, 2, 1)
+    sent, odd_offsets = lax.optimization_barrier((turned, odd_offsets))
     odd_sketch = exchanged(sent, 1)
     even_offsets = exchanged(offsets, 0)
-    even_sketch = exchanged(sketch, 0)
+    even_sketch = exchanged(turned, 0)
     blocks = blocks_of(pattern, even_offsets, offsets, odd_offsets, total)
-    return finish(blocks, even_sketch, sketch, odd_sketch, point_order)
+    return finish(blocks, even_sketch, turned, odd_sketch, point_order)
 
 
 def solution(mesh):

time: 66.9 us -> 57.7 us (0.86)
  the two profiles are of different devices: /device:TPU:5 before, /device:TPU:4 now
where the time goes in v3:
time: 57.7 us; the launch traced here: 57.6 us
  Pallas kernels  39.3 us (68%)
  starting transfers between devices  11.8 us (20%)
  waiting for transfers between devices  2.93 us (5%)
  local copies, waits for them, and re-layouts  2.92 us (5%)
  between operations  0.71 us (1%)
    pallas_call x1, Pallas kernels, blocks_of(): pl.pallas_call(functools.partial(blocks_body, total=total), in_specs=[pl....  21.5 us
    pallas_call x1, Pallas kernels, finish(): pl.pallas_call(functools.partial(finish_body, panel=panel, micro=micro),...  17.8 us
    ppermute x4, starting transfers between devices, exchanged(): return lax.ppermute(array, AXES, pairs + [(j, i) for i, j in pairs])  11.8 us
    ppermute x4, waiting for transfers between devices, exchanged(): return lax.ppermute(array, AXES, pairs + [(j, i) for i, j in pairs])  2.93 us
    unnamed x7, local copies, waits for them, and re-layouts  2.92 us
  transfers between devices with their start and end apart: 4, of which 2 were waited for; matrix products, arithmetic and copies ran while one was open for 3% of the time, Pallas kernels for 37%

profile of v3, /device:TPU:4, one launch (start us, length us, event | category | flops | bytes accessed | tf_op | source)
XLA Modules:
  0.0 57.6 jit_solution(4486441329028633730)
XLA Ops:
  0.6 5.8 %collective-permute-start.1 = (f32[3,4,512]{2,1,0:T(4,128)}, f32[3,4,512]{2,1,0:T(4,128)S(1)}, u32[]{:S(2)}, u32[]{:S(2)}) collective-permute-start(f32[3,4,512]{2,1,0:T(4,128)} %bitcast.5), channel_id=1, source_target_pairs={{1,2},{3,4},{5,6},{7,8},{9,10},{11,12},{13,14},{15,16},{17,18},{19... | collective-permute-start | bytes 73736 | tf_op jit(solution)/shard_map/ppermute | solution.py:27
  6.5 1.5 %copy.6 = bf16[4,512,256]{1,2,0:T(8,128)(2,1)S(1)} copy(bf16[4,512,256]{2,1,0:T(8,128)(2,1)} %param.5) | data formatting | bytes 2097152 | tf_op args[1]
  8.0 0.0 copy-start
  8.0 0.1 collective-permute-start.2
  8.1 1.5 %collective-permute-done.1.odd_ref = f32[3,4,512]{2,1,0:T(4,128)S(1)} collective-permute-done((f32[3,4,512]{2,1,0:T(4,128)}, f32[3,4,512]{2,1,0:T(4,128)S(1)}, u32[]{:S(2)}, u32[]{:S(2)}) %collective-permute-start.1) | collective-permute-done | bytes 24608 | tf_op jit(solution)/shard_map/ppermute | solution.py:27
  9.6 5.8 %collective-permute-start.3 = (bf16[4,256,512]{2,1,0:T(8,128)(2,1)S(1)}, bf16[4,256,512]{2,1,0:T(8,128)(2,1)S(1)}, u32[]{:S(2)}, u32[]{:S(2)}) collective-permute-start(bf16[4,256,512]{2,1,0:T(8,128)(2,1)S(1)} %bitcast.3), channel_id=1, source_target_pairs={{1,2},{3,4},{5,6},{7,8},{9,10},{11,12},{13,14},{15,16},{17,18},{19... | collective-permute-start | bytes 3145736 | tf_op jit(solution)/shard_map/ppermute | solution.py:27
  15.4 0.1 collective-permute-start
  15.5 1.4 %collective-permute-done.even_ref = f32[3,4,512]{2,1,0:T(4,128)S(1)} collective-permute-done((f32[3,4,512]{2,1,0:T(4,128)}, f32[3,4,512]{2,1,0:T(4,128)S(1)}, u32[]{:S(2)}, u32[]{:S(2)}) %collective-permute-start) | collective-permute-done | bytes 24608 | tf_op jit(solution)/shard_map/ppermute | solution.py:27
  16.9 0.0 copy-start.1
  16.9 0.7 %copy-done.1 = f32[4,3,512]{2,0,1:T(4,128)S(1)} copy-done((f32[4,3,512]{2,0,1:T(4,128)S(1)}, f32[4,3,512]{2,0,1:T(4,128)}, u32[]{:S(2)}) %copy-start.1) | copy-done | bytes 24600
  17.6 0.0 copy-start.2
  17.6 0.7 %copy-done.2 = s32[4,6]{1,0:T(4,128)S(1)} copy-done((s32[4,6]{1,0:T(4,128)S(1)}, s32[4,6]{1,0:T(4,128)}, u32[]{:S(2)}) %copy-start.2) | copy-done | bytes 120
  18.3 21.5 %blocks.1.k_ref = bf16[24,512,512]{2,1,0:T(8,128)(2,1)S(1)} custom-call(s32[4,6]{1,0:T(4,128)S(1)} %copy-done.2, f32[3,4,512]{2,1,0:T(4,128)S(1)} %collective-permute-done.even_ref, f32[3,4,512]{2,1,0:T(4,128)S(1)} %bitcast.7, f32[3,4,512]{2,1,0:T(4,128)S(1)} %collective-permute-done.1.odd_ref), custom_call_target="tpu_custom_call" | custom-call | flops 251658240 | bytes 12582912 | tf_op jit(solution)/shard_map/blocks/pallas_call | solution.py:275
  39.8 0.0 collective-permute-done.2.even_ref
  39.8 0.0 collective-permute-done.3.odd_ref
  39.8 0.0 copy-done
  39.8 17.8 %finish.1 = (bf16[4,512,256]{2,1,0:T(8,128)(2,1)}, f32[4,256,256]{2,1,0:T(8,128)}) custom-call(bf16[24,512,512]{2,1,0:T(8,128)(2,1)S(1)} %blocks.1.k_ref, bf16[4,256,512]{2,1,0:T(8,128)(2,1)S(1)} %collective-permute-done.2.even_ref, bf16[4,256,512]{2,1,0:T(8,128)(2,1)S(1)} %bitcast.4, bf16[4,256,512]{2,1,0:T(8,128)(2,1)S(1)} %collective-permute-done.3.odd_ref, ...), custom_call_target="tpu_custom_call" | custom-call | tf_op jit(solution)/shard_map/finish/pallas_call | solution.py:200
Async XLA Ops:
  0.6 9.0 %collective-permute-start.1 = (f32[3,4,512]{2,1,0:T(4,128)}, f32[3,4,512]{2,1,0:T(4,128)S(1)}, u32[]{:S(2)}, u32[]{:S(2)}) collective-permute-start(f32[3,4,512]{2,1,0:T(4,128)} %bitcast.5), channel_id=1, source_target_pairs={{1,2},{3,4},{5,6},{7,8},{9,10},{11,12},{13,14},{15,16},{17,18},{19... | collective-permute-start | bytes 73736 | tf_op jit(solution)/shard_map/ppermute | solution.py:27
  8.0 31.9 %copy-start = (s32[4,512]{1,0:T(4,128)S(1)}, s32[4,512]{1,0:T(4,128)}, u32[]{:S(2)}) copy-start(s32[4,512]{1,0:T(4,128)} %order_ref.1) | copy-start | bytes 24580
  8.0 31.8 %collective-permute-start.2 = (bf16[4,256,512]{2,1,0:T(8,128)(2,1)S(1)}, bf16[4,256,512]{2,1,0:T(8,128)(2,1)S(1)}, u32[]{:S(2)}, u32[]{:S(2)}) collective-permute-start(bf16[4,256,512]{2,1,0:T(8,128)(2,1)S(1)} %bitcast.2), channel_id=1, source_target_pairs={{0,1},{2,3},{4,5},{6,7},{8,9},{10,11},{12,13},{14,15},{16,17},{18,... | collective-permute-start | bytes 3145736 | tf_op jit(solution)/shard_map/ppermute | solution.py:27
  9.6 30.2 %collective-permute-start.3 = (bf16[4,256,512]{2,1,0:T(8,128)(2,1)S(1)}, bf16[4,256,512]{2,1,0:T(8,128)(2,1)S(1)}, u32[]{:S(2)}, u32[]{:S(2)}) collective-permute-start(bf16[4,256,512]{2,1,0:T(8,128)(2,1)S(1)} %bitcast.3), channel_id=1, source_target_pairs={{1,2},{3,4},{5,6},{7,8},{9,10},{11,12},{13,14},{15,16},{17,18},{19... | collective-permute-start | bytes 3145736 | tf_op jit(solution)/shard_map/ppermute | solution.py:27
  15.4 1.5 %collective-permute-start = (f32[3,4,512]{2,1,0:T(4,128)}, f32[3,4,512]{2,1,0:T(4,128)S(1)}, u32[]{:S(2)}, u32[]{:S(2)}) collective-permute-start(f32[3,4,512]{2,1,0:T(4,128)} %bitcast.6), channel_id=1, source_target_pairs={{0,1},{2,3},{4,5},{6,7},{8,9},{10,11},{12,13},{14,15},{16,17},{18,... | collective-permute-start | bytes 73736 | tf_op jit(solution)/shard_map/ppermute | solution.py:27
  16.9 0.7 %copy-start.1 = (f32[4,3,512]{2,0,1:T(4,128)S(1)}, f32[4,3,512]{2,0,1:T(4,128)}, u32[]{:S(2)}) copy-start(f32[4,3,512]{2,0,1:T(4,128)} %param.4) | copy-start | bytes 73732
  17.6 0.7 %copy-start.2 = (s32[4,6]{1,0:T(4,128)S(1)}, s32[4,6]{1,0:T(4,128)}, u32[]{:S(2)}) copy-start(s32[4,6]{1,0:T(4,128)} %pattern_ref.1) | copy-start | bytes 292

commit v4 on v3

--- a/solution.py
+++ b/solution.py
@@ -18,7 +18,7 @@
 softening = 0.5
 turns = wave_number / (2.0 * math.pi)
 
-SINE = (4.44288292, -7.30824569, 3.60635423, -0.84611167, 0.10982452)
+SINE = (4.44287957, -7.30781674, 3.5977744, -0.79119941)
 
 
 def exchanged(array, start):
@@ -32,18 +32,17 @@
 
 
 def kernel_values(turn_squared, points):
+    scale = turns / math.sqrt(points)
     turn = turn_squared * lax.rsqrt(turn_squared)
     part = turn - jnp.round(turn)
     square = part * part
-    sine = f32(SINE[-1])
+    sine = f32(SINE[-1] * math.sqrt(scale))
     for value in SINE[-2::-1]:
-        sine = sine * square + f32(value)
+        sine = sine * square + f32(value * math.sqrt(scale))
     sine = sine * part
-    decay = jnp.exp2(
-        turn * f32(-math.log2(math.e) / (decay_length * turns)) + f32(math.log2(turns / math.sqrt(points)))
-    )
-    level = decay * pltpu.reciprocal(turn + f32(softening * turns), approx=True)
-    return level - level * (sine * sine)
+    level = jnp.exp2(turn * f32(-math.log2(math.e) / (decay_length * turns)))
+    level = level * pltpu.reciprocal(turn + f32(softening * turns), approx=True)
+    return level * (f32(scale) - sine * sine)
 
 
 def pieces(x):
@@ -216,13 +215,19 @@
     )(*(pltpu.with_memory_space_constraint(x, pltpu.VMEM) for x in (blocks, even, own, odd)), order)
 
 
-def blocks_body(pattern_ref, even_ref, own_ref, odd_ref, out_ref, window, squares, listed, *, total):
+def blocks_body(pattern_any, even_ref, own_any, odd_ref, out_ref, window, here, there, listed, own_ref, pattern_ref, sems, *, total):
     count, points = own_ref.shape[1:]
     columns = pattern_ref.shape[1]
+    fetch_own = pltpu.make_async_copy(own_any, own_ref, sems.at[0])
+    fetch_pattern = pltpu.make_async_copy(pattern_any, pattern_ref, sems.at[1])
+    fetch_own.start()
+    fetch_pattern.start()
     me = lax.axis_index(AXES)
     first = me * count
     side = lax.rem(me, 2)
     window[...] = jnp.zeros_like(window)
+    fetch_own.wait()
+    fetch_pattern.wait()
     for group, ref in ((2 - 2 * side, even_ref), (1, own_ref), (2 * side, odd_ref)):
         for at in range(count):
             slot = group * count + at
@@ -255,15 +260,21 @@
         a, b = split_points(window[count + cluster], window[count + cluster + distance], distance)
         return contract(b, a, 0, 0)
 
-    squares[0] = measure(jnp.int32(0))
-
-    def step(at, carry):
-        after = measure(at + 1)
-        out_ref[listed[at]] = kernel_values(squares[lax.rem(at, 2)], points).astype(bf16)
-        squares[lax.rem(at + 1, 2)] = after
+    here[...] = measure(jnp.int32(0))
+
+    def two_steps(twice, carry):
+        at = 2 * twice
+        there[...] = measure(at + 1)
+        out_ref[listed[at]] = kernel_values(here[...], points).astype(bf16)
+
+        @pl.when(at + 1 < found)
+        def _():
+            here[...] = measure(at + 2)
+            out_ref[listed[at + 1]] = kernel_values(there[...], points).astype(bf16)
+
         return carry
 
-    lax.fori_loop(0, found, step, 0)
+    lax.fori_loop(0, (found + 1) // 2, two_steps, 0)
 
 
 def blocks_of(pattern, even, own, odd, total):
@@ -272,20 +283,25 @@
     pairs = count * columns
     values = pairs * points * points
     whole = pl.BlockSpec(memory_space=pltpu.VMEM)
+    far = pl.BlockSpec(memory_space=pl.ANY)
     return pl.pallas_call(
         functools.partial(blocks_body, total=total),
-        in_specs=[pl.BlockSpec(memory_space=pltpu.SMEM), whole, whole, whole],
+        in_specs=[far, whole, far, whole],
         out_specs=whole,
         scratch_shapes=[
             pltpu.VMEM((3 * count, 8, points), f32),
-            pltpu.VMEM((2, points, points), f32),
+            pltpu.VMEM((points, points), f32),
+            pltpu.VMEM((points, points), f32),
             pltpu.SMEM((pairs + 1,), jnp.int32),
+            pltpu.VMEM(own.shape, f32),
+            pltpu.SMEM(pattern.shape, jnp.int32),
+            pltpu.SemaphoreType.DMA((2,)),
         ],
         out_shape=pltpu.VMEM((pairs, points, points), bf16),
         cost_estimate=pl.CostEstimate(flops=40 * values, bytes_accessed=2 * values, transcendentals=3 * values),
         compiler_params=pltpu.CompilerParams(vmem_limit_bytes=16 * 2**20),
         name="blocks",
-    )(pattern, even, own, odd)
+    )(pltpu.with_memory_space_constraint(pattern, pltpu.HBM), even, pltpu.with_memory_space_constraint(own, pltpu.HBM), odd)
 
 
 def body(offsets, sketch, pattern, point_order):

time: 57.7 us -> 63.1 us (1.094); the launches traced: 57.6 us -> 63.9 us
  Pallas kernels: 39.3 us -> 47 us
  local copies, waits for them, and re-layouts: 2.92 us -> 1.5 us
    pallas_call x1, Pallas kernels: 21.5 us -> 29.2 us  [blocks_of(): pl.pallas_call(functools.partial(blocks_body, total=total), in_specs=[far...]
    unnamed x7 -> x3, local copies, waits for them, and re-layouts: 2.92 us -> 1.5 us
  transfers between devices with their start and end apart: 4 -> 4, of which waited for: 2 -> 2; matrix products, arithmetic and copies ran while one was open for 3% -> 2% of each run, Pallas kernels for 37% -> 46%
where the time goes in v4:
time: 63.1 us; the launch traced here: 63.9 us
  Pallas kernels  47 us (74%)
  starting transfers between devices  11.8 us (19%)
  waiting for transfers between devices  2.93 us (5%)
  local copies, waits for them, and re-layouts  1.5 us (2%)
  between operations  0.71 us (1%)
    pallas_call x1, Pallas kernels, blocks_of(): pl.pallas_call(functools.partial(blocks_body, total=total), in_specs=[far...  29.2 us
    pallas_call x1, Pallas kernels, finish(): pl.pallas_call(functools.partial(finish_body, panel=panel, micro=micro),...  17.8 us
    ppermute x4, starting transfers between devices, exchanged(): return lax.ppermute(array, AXES, pairs + [(j, i) for i, j in pairs])  11.8 us
    ppermute x4, waiting for transfers between devices, exchanged(): return lax.ppermute(array, AXES, pairs + [(j, i) for i, j in pairs])  2.93 us
    unnamed x3, local copies, waits for them, and re-layouts  1.5 us
  transfers between devices with their start and end apart: 4, of which 2 were waited for; matrix products, arithmetic and copies ran while one was open for 2% of the time, Pallas kernels for 46%

profile of v4, /device:TPU:4, one launch (start us, length us, event | category | flops | bytes accessed | tf_op | source)
XLA Modules:
  0.0 63.9 jit_solution(9687872804993397873)
XLA Ops:
  0.6 5.8 %collective-permute-start.1 = (f32[3,4,512]{2,1,0:T(4,128)}, f32[3,4,512]{2,1,0:T(4,128)S(1)}, u32[]{:S(2)}, u32[]{:S(2)}) collective-permute-start(f32[3,4,512]{2,1,0:T(4,128)} %bitcast.5), channel_id=1, source_target_pairs={{1,2},{3,4},{5,6},{7,8},{9,10},{11,12},{13,14},{15,16},{17,18},{19... | collective-permute-start | bytes 73736 | tf_op jit(solution)/shard_map/ppermute | solution.py:27
  6.5 1.5 %copy.6 = bf16[4,512,256]{1,2,0:T(8,128)(2,1)S(1)} copy(bf16[4,512,256]{2,1,0:T(8,128)(2,1)} %param.5) | data formatting | bytes 2097152 | tf_op args[1]
  8.0 0.0 copy-start
  8.0 0.1 collective-permute-start.2
  8.1 1.5 %collective-permute-done.1.odd_ref = f32[3,4,512]{2,1,0:T(4,128)S(1)} collective-permute-done((f32[3,4,512]{2,1,0:T(4,128)}, f32[3,4,512]{2,1,0:T(4,128)S(1)}, u32[]{:S(2)}, u32[]{:S(2)}) %collective-permute-start.1) | collective-permute-done | bytes 24608 | tf_op jit(solution)/shard_map/ppermute | solution.py:27
  9.6 5.8 %collective-permute-start.3 = (bf16[4,256,512]{2,1,0:T(8,128)(2,1)S(1)}, bf16[4,256,512]{2,1,0:T(8,128)(2,1)S(1)}, u32[]{:S(2)}, u32[]{:S(2)}) collective-permute-start(bf16[4,256,512]{2,1,0:T(8,128)(2,1)S(1)} %bitcast.3), channel_id=1, source_target_pairs={{1,2},{3,4},{5,6},{7,8},{9,10},{11,12},{13,14},{15,16},{17,18},{19... | collective-permute-start | bytes 3145736 | tf_op jit(solution)/shard_map/ppermute | solution.py:27
  15.4 0.1 collective-permute-start
  15.5 1.4 %collective-permute-done.even_ref = f32[3,4,512]{2,1,0:T(4,128)S(1)} collective-permute-done((f32[3,4,512]{2,1,0:T(4,128)}, f32[3,4,512]{2,1,0:T(4,128)S(1)}, u32[]{:S(2)}, u32[]{:S(2)}) %collective-permute-start) | collective-permute-done | bytes 24608 | tf_op jit(solution)/shard_map/ppermute | solution.py:27
  16.9 29.2 %blocks.1.k_ref = bf16[24,512,512]{2,1,0:T(8,128)(2,1)S(1)} custom-call(s32[4,6]{1,0:T(4,128)} %pattern_any.1, f32[3,4,512]{2,1,0:T(4,128)S(1)} %collective-permute-done.even_ref, f32[3,4,512]{2,1,0:T(4,128)} %bitcast.7, f32[3,4,512]{2,1,0:T(4,128)S(1)} %collective-permute-done.1.odd_ref), custom_call_target="tpu_custom_call" | custom-call | flops 251658240 | bytes 12582912 | tf_op jit(solution)/shard_map/blocks/pallas_call | solution.py:287
  46.1 0.0 collective-permute-done.2.even_ref
  46.1 0.0 collective-permute-done.3.odd_ref
  46.1 0.0 copy-done
  46.1 17.8 %finish.1 = (bf16[4,512,256]{2,1,0:T(8,128)(2,1)}, f32[4,256,256]{2,1,0:T(8,128)}) custom-call(bf16[24,512,512]{2,1,0:T(8,128)(2,1)S(1)} %blocks.1.k_ref, bf16[4,256,512]{2,1,0:T(8,128)(2,1)S(1)} %collective-permute-done.2.even_ref, bf16[4,256,512]{2,1,0:T(8,128)(2,1)S(1)} %bitcast.4, bf16[4,256,512]{2,1,0:T(8,128)(2,1)S(1)} %collective-permute-done.3.odd_ref, ...), custom_call_target="tpu_custom_call" | custom-call | tf_op jit(solution)/shard_map/finish/pallas_call | solution.py:199
Async XLA Ops:
  0.6 9.0 %collective-permute-start.1 = (f32[3,4,512]{2,1,0:T(4,128)}, f32[3,4,512]{2,1,0:T(4,128)S(1)}, u32[]{:S(2)}, u32[]{:S(2)}) collective-permute-start(f32[3,4,512]{2,1,0:T(4,128)} %bitcast.5), channel_id=1, source_target_pairs={{1,2},{3,4},{5,6},{7,8},{9,10},{11,12},{13,14},{15,16},{17,18},{19... | collective-permute-start | bytes 73736 | tf_op jit(solution)/shard_map/ppermute | solution.py:27
  8.0 38.1 %copy-start = (s32[4,512]{1,0:T(4,128)S(1)}, s32[4,512]{1,0:T(4,128)}, u32[]{:S(2)}) copy-start(s32[4,512]{1,0:T(4,128)} %order_ref.1) | copy-start | bytes 24580
  8.0 38.1 %collective-permute-start.2 = (bf16[4,256,512]{2,1,0:T(8,128)(2,1)S(1)}, bf16[4,256,512]{2,1,0:T(8,128)(2,1)S(1)}, u32[]{:S(2)}, u32[]{:S(2)}) collective-permute-start(bf16[4,256,512]{2,1,0:T(8,128)(2,1)S(1)} %bitcast.2), channel_id=1, source_target_pairs={{0,1},{2,3},{4,5},{6,7},{8,9},{10,11},{12,13},{14,15},{16,17},{18,... | collective-permute-start | bytes 3145736 | tf_op jit(solution)/shard_map/ppermute | solution.py:27
  9.6 36.5 %collective-permute-start.3 = (bf16[4,256,512]{2,1,0:T(8,128)(2,1)S(1)}, bf16[4,256,512]{2,1,0:T(8,128)(2,1)S(1)}, u32[]{:S(2)}, u32[]{:S(2)}) collective-permute-start(bf16[4,256,512]{2,1,0:T(8,128)(2,1)S(1)} %bitcast.3), channel_id=1, source_target_pairs={{1,2},{3,4},{5,6},{7,8},{9,10},{11,12},{13,14},{15,16},{17,18},{19... | collective-permute-start | bytes 3145736 | tf_op jit(solution)/shard_map/ppermute | solution.py:27
  15.4 1.5 %collective-permute-start = (f32[3,4,512]{2,1,0:T(4,128)}, f32[3,4,512]{2,1,0:T(4,128)S(1)}, u32[]{:S(2)}, u32[]{:S(2)}) collective-permute-start(f32[3,4,512]{2,1,0:T(4,128)} %bitcast.6), channel_id=1, source_target_pairs={{0,1},{2,3},{4,5},{6,7},{8,9},{10,11},{12,13},{14,15},{16,17},{18,... | collective-permute-start | bytes 73736 | tf_op jit(solution)/shard_map/ppermute | solution.py:27

commit v5 on v4

--- a/solution.py
+++ b/solution.py
@@ -85,13 +85,26 @@
 def factor_panel(rows, ups, first, panel, micro):
     half = first // 128
     base = first % 128
+    pair = micro // 2
     lanes = lax.broadcasted_iota(jnp.int32, (8, 128), 1)
+    lower = lax.broadcasted_iota(jnp.int32, (8, 128), 0) < 4
+
+    def packed(x, y):
+        return jnp.where(lower, x, pltpu.roll(y, 4, axis=0))
+
     for start in range(0, panel, micro):
         lane0 = base + start
         inside = (lanes >= lane0) & (lanes < lane0 + micro)
         raw = [rows[half, 8 * (start + j):8 * (start + j) + 8, :] for j in range(micro)]
         other = [rows[1 - half, 8 * (start + j):8 * (start + j) + 8, :] for j in range(micro)]
-        a = [[lane_of(raw[i], lane0 + k) for k in range(i + 1)] for i in range(micro)]
+        a = [[None] * micro for _ in range(micro)]
+        for i in range(pair):
+            both = packed(raw[i], raw[i + pair])
+            for k in range(i + pair + 1):
+                value = lane_of(both, lane0 + k)
+                if k <= i:
+                    a[i][k] = value
+                a[i + pair][k] = pltpu.roll(value, 4, axis=0)
         low = [[None] * micro for _ in range(micro)]
         inv = [None] * micro
         for k in range(micro):
@@ -115,17 +128,21 @@
             ups[at, :] = raw[j]
             rows[half, at, :] = solved[j]
             rows[1 - half, at, :] = other[j]
+        if start + micro < panel:
+            raw = [packed(raw[j], raw[j + pair]) for j in range(pair)]
+            solved = [packed(solved[j], solved[j + pair]) for j in range(pair)]
+            other = [packed(other[j], other[j + pair]) for j in range(pair)]
         for i in range(start + micro, panel):
             at = slice(8 * i, 8 * i + 8)
             x = jnp.where(inside, f32(0), rows[half, at, :])
             y = rows[1 - half, at, :]
             tx = ty = None
-            for j in range(micro):
+            for j in range(pair):
                 c = lane_of(raw[j], base + i)
                 tx = c * solved[j] if tx is None else tx + c * solved[j]
                 ty = c * other[j] if ty is None else ty + c * other[j]
-            rows[half, at, :] = x - tx
-            rows[1 - half, at, :] = y - ty
+            rows[half, at, :] = x - (tx + pltpu.roll(tx, 4, axis=0))
+            rows[1 - half, at, :] = y - (ty + pltpu.roll(ty, 4, axis=0))
 
 def finish_body(k_ref, even_ref, own_ref, odd_ref, order_ref, basis_ref, factor_ref, t_ref, mat, inv_ref, rows, ups, *, panel, micro):
     count, width, points = own_ref.shape
@@ -193,7 +210,7 @@
         pick = jnp.concatenate([jnp.where(order_t == place + f32(128 * q), f32(1), f32(0)).astype(bf16) for q in range(points // 128)], axis=1)
         basis_ref[c] = contract(pick, b, 1, 1).astype(bf16)
 
-def finish(blocks, even, own, odd, order, panel=16, micro=8):
+def finish(blocks, even, own, odd, order, panel=32, micro=8):
     count, width, points = own.shape
     whole = pl.BlockSpec(memory_space=pltpu.VMEM)
     return pl.pallas_call(
@@ -266,15 +283,15 @@
         at = 2 * twice
         there[...] = measure(at + 1)
         out_ref[listed[at]] = kernel_values(here[...], points).astype(bf16)
-
-        @pl.when(at + 1 < found)
-        def _():
-            here[...] = measure(at + 2)
-            out_ref[listed[at + 1]] = kernel_values(there[...], points).astype(bf16)
-
+        here[...] = measure(at + 2)
+        out_ref[listed[at + 1]] = kernel_values(there[...], points).astype(bf16)
         return carry
 
-    lax.fori_loop(0, (found + 1) // 2, two_steps, 0)
+    lax.fori_loop(0, found // 2, two_steps, 0)
+
+    @pl.when(lax.rem(found, 2) == 1)
+    def _():
+        out_ref[listed[found - 1]] = kernel_values(here[...], points).astype(bf16)
 
 
 def blocks_of(pattern, even, own, odd, total):

time: 63.1 us -> 51.1 us (0.81)
  the two profiles are of different devices: /device:TPU:4 before, /device:TPU:6 now
where the time goes in v5:
time: 51.1 us; the launch traced here: 50.9 us
  Pallas kernels  34.6 us (68%)
  starting transfers between devices  8.31 us (16%)
  waiting for transfers between devices  5.8 us (11%)
  local copies, waits for them, and re-layouts  1.5 us (3%)
  between operations  0.69 us (1%)
    pallas_call x1, Pallas kernels, blocks_of(): pl.pallas_call(functools.partial(blocks_body, total=total), in_specs=[far...  18 us
    pallas_call x1, Pallas kernels, finish(): pl.pallas_call(functools.partial(finish_body, panel=panel, micro=micro),...  16.6 us
    ppermute x4, starting transfers between devices, exchanged(): return lax.ppermute(array, AXES, pairs + [(j, i) for i, j in pairs])  8.31 us
    ppermute x4, waiting for transfers between devices, exchanged(): return lax.ppermute(array, AXES, pairs + [(j, i) for i, j in pairs])  5.8 us
    unnamed x3, local copies, waits for them, and re-layouts  1.5 us
  transfers between devices with their start and end apart: 4, of which 3 were waited for; matrix products, arithmetic and copies ran while one was open for 3% of the time, Pallas kernels for 35%

profile of v5, /device:TPU:6, one launch (start us, length us, event | category | flops | bytes accessed | tf_op | source)
XLA Modules:
  0.0 50.9 jit_solution(3504715371101933718)
XLA Ops:
  0.6 1.9 %collective-permute-start.1 = (f32[3,4,512]{2,1,0:T(4,128)}, f32[3,4,512]{2,1,0:T(4,128)S(1)}, u32[]{:S(2)}, u32[]{:S(2)}) collective-permute-start(f32[3,4,512]{2,1,0:T(4,128)} %bitcast.5), channel_id=1, source_target_pairs={{1,2},{3,4},{5,6},{7,8},{9,10},{11,12},{13,14},{15,16},{17,18},{19... | collective-permute-start | bytes 73736 | tf_op jit(solution)/shard_map/ppermute | solution.py:27
  2.6 1.5 %copy.6 = bf16[4,512,256]{1,2,0:T(8,128)(2,1)S(1)} copy(bf16[4,512,256]{2,1,0:T(8,128)(2,1)} %param.5) | data formatting | bytes 2097152 | tf_op args[1]
  4.1 0.0 copy-start
  4.1 1.7 %collective-permute-start.2 = (bf16[4,256,512]{2,1,0:T(8,128)(2,1)S(1)}, bf16[4,256,512]{2,1,0:T(8,128)(2,1)S(1)}, u32[]{:S(2)}, u32[]{:S(2)}) collective-permute-start(bf16[4,256,512]{2,1,0:T(8,128)(2,1)S(1)} %bitcast.2), channel_id=1, source_target_pairs={{0,1},{2,3},{4,5},{6,7},{8,9},{10,11},{12,13},{14,15},{16,17},{18,... | collective-permute-start | bytes 3145736 | tf_op jit(solution)/shard_map/ppermute | solution.py:27
  5.8 0.2 collective-permute-done.1.odd_ref
  6.0 4.6 %collective-permute-start.3 = (bf16[4,256,512]{2,1,0:T(8,128)(2,1)S(1)}, bf16[4,256,512]{2,1,0:T(8,128)(2,1)S(1)}, u32[]{:S(2)}, u32[]{:S(2)}) collective-permute-start(bf16[4,256,512]{2,1,0:T(8,128)(2,1)S(1)} %bitcast.3), channel_id=1, source_target_pairs={{1,2},{3,4},{5,6},{7,8},{9,10},{11,12},{13,14},{15,16},{17,18},{19... | collective-permute-start | bytes 3145736 | tf_op jit(solution)/shard_map/ppermute | solution.py:27
  10.6 0.1 collective-permute-start
  10.7 1.4 %collective-permute-done.even_ref = f32[3,4,512]{2,1,0:T(4,128)S(1)} collective-permute-done((f32[3,4,512]{2,1,0:T(4,128)}, f32[3,4,512]{2,1,0:T(4,128)S(1)}, u32[]{:S(2)}, u32[]{:S(2)}) %collective-permute-start) | collective-permute-done | bytes 24608 | tf_op jit(solution)/shard_map/ppermute | solution.py:27
  12.1 18.0 %blocks.1.k_ref = bf16[24,512,512]{2,1,0:T(8,128)(2,1)S(1)} custom-call(s32[4,6]{1,0:T(4,128)} %pattern_any.1, f32[3,4,512]{2,1,0:T(4,128)S(1)} %collective-permute-done.even_ref, f32[3,4,512]{2,1,0:T(4,128)} %bitcast.7, f32[3,4,512]{2,1,0:T(4,128)S(1)} %collective-permute-done.1.odd_ref), custom_call_target="tpu_custom_call" | custom-call | flops 251658240 | bytes 12582912 | tf_op jit(solution)/shard_map/blocks/pallas_call | solution.py:304
  30.1 0.0 collective-permute-done.2.even_ref
  30.1 4.2 %collective-permute-done.3.odd_ref = bf16[4,256,512]{2,1,0:T(8,128)(2,1)S(1)} collective-permute-done((bf16[4,256,512]{2,1,0:T(8,128)(2,1)S(1)}, bf16[4,256,512]{2,1,0:T(8,128)(2,1)S(1)}, u32[]{:S(2)}, u32[]{:S(2)}) %collective-permute-start.3) | collective-permute-done | bytes 1048608 | tf_op jit(solution)/shard_map/ppermute | solution.py:27
  34.3 0.0 copy-done
  34.3 16.6 %finish.1 = (bf16[4,512,256]{2,1,0:T(8,128)(2,1)}, f32[4,256,256]{2,1,0:T(8,128)}) custom-call(bf16[24,512,512]{2,1,0:T(8,128)(2,1)S(1)} %blocks.1.k_ref, bf16[4,256,512]{2,1,0:T(8,128)(2,1)S(1)} %collective-permute-done.2.even_ref, bf16[4,256,512]{2,1,0:T(8,128)(2,1)S(1)} %bitcast.4, bf16[4,256,512]{2,1,0:T(8,128)(2,1)S(1)} %collective-permute-done.3.odd_ref, ...), custom_call_target="tpu_custom_call" | custom-call | tf_op jit(solution)/shard_map/finish/pallas_call | solution.py:216
Async XLA Ops:
  0.6 5.4 %collective-permute-start.1 = (f32[3,4,512]{2,1,0:T(4,128)}, f32[3,4,512]{2,1,0:T(4,128)S(1)}, u32[]{:S(2)}, u32[]{:S(2)}) collective-permute-start(f32[3,4,512]{2,1,0:T(4,128)} %bitcast.5), channel_id=1, source_target_pairs={{1,2},{3,4},{5,6},{7,8},{9,10},{11,12},{13,14},{15,16},{17,18},{19... | collective-permute-start | bytes 73736 | tf_op jit(solution)/shard_map/ppermute | solution.py:27
  4.1 30.2 %copy-start = (s32[4,512]{1,0:T(4,128)S(1)}, s32[4,512]{1,0:T(4,128)}, u32[]{:S(2)}) copy-start(s32[4,512]{1,0:T(4,128)} %order_ref.1) | copy-start | bytes 24580
  4.1 26.0 %collective-permute-start.2 = (bf16[4,256,512]{2,1,0:T(8,128)(2,1)S(1)}, bf16[4,256,512]{2,1,0:T(8,128)(2,1)S(1)}, u32[]{:S(2)}, u32[]{:S(2)}) collective-permute-start(bf16[4,256,512]{2,1,0:T(8,128)(2,1)S(1)} %bitcast.2), channel_id=1, source_target_pairs={{0,1},{2,3},{4,5},{6,7},{8,9},{10,11},{12,13},{14,15},{16,17},{18,... | collective-permute-start | bytes 3145736 | tf_op jit(solution)/shard_map/ppermute | solution.py:27
  6.0 28.3 %collective-permute-start.3 = (bf16[4,256,512]{2,1,0:T(8,128)(2,1)S(1)}, bf16[4,256,512]{2,1,0:T(8,128)(2,1)S(1)}, u32[]{:S(2)}, u32[]{:S(2)}) collective-permute-start(bf16[4,256,512]{2,1,0:T(8,128)(2,1)S(1)} %bitcast.3), channel_id=1, source_target_pairs={{1,2},{3,4},{5,6},{7,8},{9,10},{11,12},{13,14},{15,16},{17,18},{19... | collective-permute-start | bytes 3145736 | tf_op jit(solution)/shard_map/ppermute | solution.py:27
  10.6 1.5 %collective-permute-start = (f32[3,4,512]{2,1,0:T(4,128)}, f32[3,4,512]{2,1,0:T(4,128)S(1)}, u32[]{:S(2)}, u32[]{:S(2)}) collective-permute-start(f32[3,4,512]{2,1,0:T(4,128)} %bitcast.6), channel_id=1, source_target_pairs={{0,1},{2,3},{4,5},{6,7},{8,9},{10,11},{12,13},{14,15},{16,17},{18,... | collective-permute-start | bytes 73736 | tf_op jit(solution)/shard_map/ppermute | solution.py:27
